TPU v7x, 128 devices: a whole 4x4x4 slice. The times are simulated.
128 devices in a mesh: row: 4 (over y), col: 32 (over x, z, core).
Axes of the slice: x: 4, y: 4, z: 4, core: 2. Of those that a mesh axis runs over, the one named last changes fastest.
Arguments:
- cov: float32 [18432, 18432], P('row', 'col'), may hold values from -1 to 70, as said below
- weights: float32 [18432], P(('row', 'col')), may hold values from -0.6 to 0.6
- act: bfloat16 [8, 2048, 144], P('row', 'col'), may hold values from -6 to 6
- upstream: bfloat16 [8, 2048, 128], P('row', 'col'), may hold values from -6 to 6
- neighbors: int32 [8, 2048, 138], P('row', 'col'), may hold values from 0 to 2047
- types: int32 [8, 2048], P('row', 'col'), may hold values from 0 to 1
- type_gain: float32 [2, 128], replicated, may hold values from 0.25 to 1.75
- sens: float32 [64, 2048], P('row', 'col'), may hold values from -0.00048828125 to 0.00048828125
- frame_for_measure: int32 [64], P('row'), may hold values from 0 to 1
- noise_variance: float32 [64], replicated, may hold values from 0.5 to 2
- innovation: float32 [64], replicated, may hold values from -6 to 6
Outputs:
- weights_new: float32 [18432], P(('row', 'col'))
- cov_new: float32 [18432, 18432], P('row', 'col')
Inputs may be any that keep to these rules, and one draw needn't show every extreme that they name: cov is symmetric and positive definite.
All inputs are finite; a program needn't handle non-finite values. Where the computation divides by a largest or mean magnitude, that divisor is 1e-20 or more.
Results may differ from a plain program's by a relative error of at most 0.0023.
Values may be sent and summed in bfloat16 or wider, within the bound.
A program may use at most 128 MiB of HBM per device.

v0:
```python
import math

import jax
import jax.numpy as jnp
from jax import lax
from jax.sharding import PartitionSpec as P

NS_ITERS = 5


FULL_PRECISION = lax.Precision.HIGHEST


def spread(block, axis, holder):
    block = jnp.where(lax.axis_index(axis) == holder, block, jnp.zeros_like(block))
    return lax.psum(block, axis)


def matmul(left, right):
    return jnp.dot(left, right, precision=FULL_PRECISION)


def on_device(
    cov,
    weights,
    act,
    upstream,
    neighbors,
    types,
    type_gain,
    sens,
    frame_for_measure,
    noise_variance,
    innovation,
):
    row_count_local = lax.axis_size("row")
    column_count_local = lax.axis_size("col")
    col_index = lax.axis_index("col")
    measure_local = sens.shape[0]
    measure_overall = measure_local * row_count_local
    col_width = cov.shape[1]
    subblock_width = weights.shape[0]
    per_block = column_count_local // row_count_local
    whole_up = lax.all_gather(upstream, "col", axis=1, tiled=True)
    picked = jax.vmap(lambda lookup, indices: jnp.take(lookup, indices, axis=0))(
        whole_up, neighbors
    )
    neighbor_sum = jnp.sum(picked, axis=2, dtype=jnp.float32) * (
        1.0 / math.sqrt(neighbors.shape[2])
    )
    type_hot = (
        types[:, :, None] == jnp.arange(type_gain.shape[0], dtype=jnp.int32)[None, None, :]
    ).astype(jnp.float32)
    type_scale = jnp.einsum("fit,tb->fib", type_hot, type_gain, precision=FULL_PRECISION)
    adjoint = type_scale * (upstream.astype(jnp.float32) + neighbor_sum)
    chosen_adjoint = jnp.take(adjoint, frame_for_measure, axis=0)
    weighted = (sens[:, :, None] * chosen_adjoint).astype(jnp.bfloat16)
    chosen_act = jnp.take(act, frame_for_measure, axis=0)
    partial_jacobian = jnp.einsum(
        "mib,mia->mba", weighted, chosen_act, preferred_element_type=jnp.float32
    )
    partial_jacobian = partial_jacobian.reshape(
        measure_local, row_count_local, column_count_local, subblock_width
    )
    summed = lax.psum_scatter(partial_jacobian, "col", scatter_dimension=2, tiled=True)
    grouped_again = lax.all_to_all(summed, "row", split_axis=1, concat_axis=0, tiled=True)
    jacobian_subblock = grouped_again.reshape(measure_overall, subblock_width)
    jac_rows = lax.all_gather(jacobian_subblock, "col", axis=1, tiled=True)
    owner_piece = lax.dynamic_slice_in_dim(
        jac_rows, col_index % per_block * col_width, col_width, 1
    )
    jac_cols = spread(owner_piece, "row", col_index // per_block)
    numerator_sub = lax.psum_scatter(
        lax.dot_general(cov, jac_cols, (((1,), (1,)), ((), ())), precision=FULL_PRECISION),
        "col",
        scatter_dimension=0,
        tiled=True,
    )
    innovation_cov = lax.psum(matmul(jacobian_subblock, numerator_sub), ("row", "col")) + jnp.diag(
        noise_variance
    )
    scale_factor = 1.0 / jnp.max(jnp.sum(jnp.abs(innovation_cov), axis=1))
    identity_matrix = jnp.eye(measure_overall, dtype=jnp.float32)
    inverse_matrix = identity_matrix * scale_factor
    for sweep in range(NS_ITERS):
        inverse_matrix = 2.0 * inverse_matrix - matmul(
            matmul(inverse_matrix, innovation_cov), inverse_matrix
        )
    gain_sub = matmul(numerator_sub, inverse_matrix)
    weights_new = weights + matmul(gain_sub, innovation)
    gain_block = lax.all_gather(gain_sub.astype(jnp.bfloat16), "col", axis=0, tiled=True).astype(
        gain_sub.dtype
    )
    column_part = matmul(jac_rows, cov)
    column_total = lax.psum(column_part.astype(jnp.bfloat16), "row").astype(jnp.float32)
    cov_new = cov - matmul(gain_block, column_total)
    return (weights_new, cov_new)


def solution(mesh):
    return jax.shard_map(
        on_device,
        mesh=mesh,
        in_specs=(
            P("row", "col"),
            P(("row", "col")),
            P("row", "col", None),
            P("row", "col", None),
            P("row", "col", None),
            P("row", "col"),
            P(),
            P("row", "col"),
            P("row"),
            P(),
            P(),
        ),
        out_specs=(P(("row", "col")), P("row", "col")),
        check_vma=False,
    )
```

profile of v0, /device:TPU:1, one launch (start us, length us, event | category | flops | bytes accessed | tf_op | source)
XLA Modules:
  0.0 654.8 jit_solution(4610884836985850745)
XLA Ops:
  7.2 0.0 copy-start
  7.2 0.0 all-gather.5.cloned.1.call-start
  7.2 0.7 all-gather.5.cloned.1.call-update
  7.9 0.0 reduce-scatter.5.cloned.1.call-start
  8.0 0.9 bitcast_or_fusion
  8.9 0.2 reshape.42
  9.1 0.7 compare_select_fusion.1
  9.8 0.6 gather_fusion.1
  10.4 0.7 compare_and_fusion.1
  11.0 0.9 compare_and_fusion
  12.0 45.0 %all-gather.5.cloned.1.call-done = bf16[2,2048,128]{2,1,0:T(8,128)(2,1)} async-done(((bf16[2,64,128]{2,1,0:T(8,128)(2,1)}), bf16[2,2048,128]{2,1,0:T(8,128)(2,1)}) %all-gather.5.cloned.1.call-update) | async-done | bytes 1048592 | tf_op jit(solution)/shard_map/all_gather | solution.py:44
  57.0 197.2 %gather_fusion.2 = bf16[17664,128]{1,0:T(8,128)(2,1)} fusion(bf16[2,2048,128]{2,1,0:T(8,128)(2,1)} %all-gather.5.cloned.1.call-done, s32[17664]{0:T(1024)S(1)} %reshape.42), kind=kCustom, calls=%fused_computation.2 | custom fusion | bytes 9185280 | tf_op jit(solution)/shard_map/vmap(jit(_take))/gather | solution.py:45
  254.2 7.2 %reshape.45 = bf16[2,64,138,128]{3,2,1,0:T(8,128)(2,1)} reshape(bf16[17664,128]{1,0:T(8,128)(2,1)} %gather_fusion.2) | data formatting | bytes 9043968 | tf_op jit(solution)/shard_map/vmap(jit(_take))/gather | solution.py:45
  261.4 8.2 %convert_reduce_fusion = f32[2,64,128]{2,1,0:T(8,128)S(1)} fusion(bf16[2,64,138,128]{3,2,1,0:T(8,128)(2,1)} %reshape.45, pred[2,64,138]{2,1,0:T(8,128)(4,1)S(1)} %compare_and_fusion), kind=kLoop, calls=%fused_computation.3 | loop fusion | flops 6766592 | bytes 4605184 | tf_op jit(solution)/shard_map/reduce_sum | solution.py:48
  269.6 0.2 convolution_multiply_fusion
  269.9 0.6 gather_fusion
  270.5 0.8 fusion
  271.3 2.5 copy.21
  273.8 0.0 reduce-scatter.5.cloned.1.call-update
  273.8 0.0 all-gather.7.cloned.1.call-start
  273.9 76.2 %reduce-scatter.5.cloned.1.call-done = f32[16,4,1,144]{3,0,1,2:T(8,128)} async-done(((f32[16,4,32,144]{3,0,1,2:T(8,128)}), f32[16,4,1,144]{3,0,1,2:T(8,128)}) %reduce-scatter.5.cloned.1.call-update) | async-done | bytes 36880 | tf_op jit(solution)/shard_map/reduce_scatter | solution.py:65
  350.1 0.9 copy.22
  351.0 8.3 %all_to_all.15 = f32[16,4,1,144]{3,2,0,1:T(1,128)S(1)} all-to-all(f32[16,4,1,144]{3,2,0,1:T(1,128)S(1)} %copy.22), channel_id=1, replica_groups=mesh['row'=4,'col'=32] {'row'}, dimensions={1} | all-to-all | bytes 73728 | tf_op jit(solution)/shard_map/all_to_all | solution.py:66
  359.3 0.6 copy.28
  360.0 0.0 all-gather.7.cloned.1.call-update
  360.0 0.0 all-reduce.3.cloned.1.call-start
  360.1 44.9 %all-gather.7.cloned.1.call-done = f32[32,144,64]{1,2,0:T(8,128)} async-done(((f32[1,144,64]{1,2,0:T(8,128)}), f32[32,144,64]{1,2,0:T(8,128)}) %all-gather.7.cloned.1.call-update) | async-done | bytes 1179664 | tf_op jit(solution)/shard_map/all_gather | solution.py:68
  404.9 2.8 copy.23
  407.7 1.6 reshape.56
  409.4 0.8 select_bitcast_fusion
  410.1 0.0 all-reduce.3.cloned.1.call-update
  410.2 0.0 reduce-scatter.7.cloned.1.call-start
  410.2 38.2 %all-reduce.3.cloned.1.call-done = f32[64,576]{1,0:T(8,128)} async-done(((f32[64,576]{1,0:T(8,128)}), f32[64,576]{1,0:T(8,128)}) %all-reduce.3.cloned.1.call-update) | async-done | bytes 147472 | tf_op jit(solution)/shard_map/psum | solution.py:16
  448.4 9.4 %convolution_bitcast_fusion = f32[4608,64]{0,1:T(8,128)S(1)} fusion(f32[64,576]{1,0:T(8,128)} %all-reduce.3.cloned.1.call-done, f32[4608,576]{0,1:T(8,128)} %param.11), kind=kOutput, calls=%fused_computation.5 | convolution fusion | flops 2038431744 | bytes 11943936 | tf_op jit(solution)/shard_map/dot_general | solution.py:74
  457.8 0.0 copy-start.3
  457.9 0.0 copy-start.8
  457.9 1.9 copy.26
  459.7 0.0 reduce-scatter.7.cloned.1.call-update
  459.8 0.0 copy-start.5
  459.8 0.2 all-reduce.5.cloned.1.call-start
  460.0 12.7 %convolution_convert_fusion = bf16[64,576]{1,0:T(8,128)(2,1)} fusion(f32[4608,64]{0,1:T(8,128)S(1)} %reshape.56, f32[4608,576]{0,1:T(8,128)} %param.11), kind=kOutput, calls=%fused_computation.6 | convolution fusion | flops 2038468608 | bytes 11870208 | tf_op jit(solution)/shard_map/dot_general | solution.py:20
  472.7 0.0 all-reduce.5.cloned.1.call-update
  472.7 67.4 %reduce-scatter.7.cloned.1.call-done = f32[144,64]{1,0:T(8,128)} async-done(((f32[4608,64]{1,0:T(8,128)}), f32[144,64]{1,0:T(8,128)}) %reduce-scatter.7.cloned.1.call-update) | async-done | bytes 36880
  540.2 1.1 fusion.28
  541.3 66.1 %psum.22 = f32[64,64]{1,0:T(8,128)S(1)} all-reduce(f32[64,64]{1,0:T(8,128)S(1)} %fusion.28), channel_id=1, replica_groups=mesh['row'=4,'col'=32] {'row','col'}, use_global_device_ids=true, to_apply=%region_4.5 | all-reduce | flops 4096 | bytes 32768 | tf_op jit(solution)/shard_map/psum | solution.py:79
  607.3 0.2 abs_reduce_fusion
  607.5 0.6 reduce_max.9
  608.8 0.2 fusion.8
  609.1 0.2 convolution_subtract_fusion.5
  609.2 0.2 fusion.27
  609.5 0.2 convolution_subtract_fusion.4
  609.6 0.2 fusion.26
  609.9 0.2 convolution_subtract_fusion.3
  610.1 0.2 fusion.25
  610.3 0.2 convolution_subtract_fusion.2
  610.5 0.2 fusion.24
  610.7 0.2 convolution_subtract_fusion.1
  610.9 1.2 fusion.29
  612.1 0.1 fusion.18
  612.2 23.1 %all-gather.1 = bf16[32,144,64]{1,2,0:T(8,128)(2,1)S(1)} all-gather(bf16[1,144,64]{1,2,0:T(8,128)(2,1)S(1)} %convert_bitcast_fusion), channel_id=1, replica_groups=mesh['row'=4,'col'=32] {'col'}, dimensions={0}, use_global_device_ids=true | all-gather | bytes 608256 | tf_op jit(solution)/shard_map/all_gather | solution.py:91
  635.3 0.6 copy.24
  635.9 1.7 reshape.58
  637.6 0.6 add.48
  638.2 9.8 %convolution_subtract_fusion = f32[4608,576]{0,1:T(8,128)} fusion(f32[4608,576]{0,1:T(8,128)} %param.11, bf16[4608,64]{0,1:T(8,128)(2,1)S(1)} %reshape.58, bf16[64,576]{1,0:T(8,128)(2,1)} %all-reduce.5.cloned.1.call-done), kind=kOutput, calls=%fused_computation.4 | convolution fusion | flops 342392832 | bytes 21897216 | tf_op jit(solution)/shard_map/dot_general | solution.py:20
  (17 shorter events, 0.0 us)
Async XLA Ops:
  7.2 2.6 copy-start
  7.2 49.8 %all-gather.5.cloned.1.call-start = ((), (), s32[]{:S(2)}) async-start(), calls=%async_computation.3 | async-start | bytes 1081344 | tf_op jit(solution)/shard_map/all_gather | solution.py:44
  7.9 342.2 %reduce-scatter.5.cloned.1.call-start = ((), (), s32[]{:S(2)}) async-start(), calls=%async_computation.4 | async-start | bytes 2162688 | tf_op jit(solution)/shard_map/reduce_scatter | solution.py:65
  254.2 15.5 %copy-start.2 = (bf16[2,64,128]{2,1,0:T(8,128)(2,1)S(1)}, bf16[2,64,128]{2,1,0:T(8,128)(2,1)}, u32[]{:S(2)}) copy-start(bf16[2,64,128]{2,1,0:T(8,128)(2,1)} %param.14) | copy-start | bytes 98308
  254.2 15.5 %copy-start.6 = (f32[2,128]{1,0:T(2,128)S(1)}, f32[2,128]{1,0:T(2,128)}, u32[]{:S(2)}) copy-start(f32[2,128]{1,0:T(2,128)} %param.17) | copy-start | bytes 3076
  254.2 15.5 %copy-start.7 = (s32[2,64]{1,0:T(2,128)S(1)}, s32[2,64]{1,0:T(2,128)}, u32[]{:S(2)}) copy-start(s32[2,64]{1,0:T(2,128)} %param.16) | copy-start | bytes 1540
  254.2 16.3 %copy-start.4 = (f32[16,64]{1,0:T(8,128)S(1)}, f32[16,64]{1,0:T(8,128)}, u32[]{:S(2)}) copy-start(f32[16,64]{1,0:T(8,128)} %param.18) | copy-start | bytes 12292
  273.8 131.1 %all-gather.7.cloned.1.call-start = ((), (), s32[]{:S(2)}) async-start(), calls=%async_computation.7 | async-start | bytes 2162688 | tf_op jit(solution)/shard_map/all_gather | solution.py:68
  360.0 88.4 %all-reduce.3.cloned.1.call-start = ((), (), s32[]{:S(2)}) async-start(), calls=%async_computation.5 | async-start | bytes 327680 | tf_op jit(solution)/shard_map/psum | solution.py:16
  410.2 130.0 %reduce-scatter.7.cloned.1.call-start = ((), (), s32[]{:S(2)}) async-start(), calls=%async_computation.8 | async-start | bytes 2433024
  457.8 82.3 %copy-start.1 = (f32[16,4,1,144]{3,0,2,1:T(8,128)S(1)}, f32[16,4,1,144]{3,0,2,1:T(8,128)}, u32[]{:S(2)}) copy-start(f32[16,4,1,144]{3,0,2,1:T(8,128)} %copy.28) | copy-start | bytes 110596
  457.8 149.5 %copy-start.3 = (f32[64]{0:T(128)S(1)}, f32[64]{0:T(128)}, u32[]{:S(2)}) copy-start(f32[64]{0:T(128)} %param.20) | copy-start | bytes 772
  457.9 154.2 %copy-start.8 = (f32[64]{0:T(128)S(1)}, f32[64]{0:T(128)}, u32[]{:S(2)}) copy-start(f32[64]{0:T(128)} %param.21) | copy-start | bytes 772
  459.8 177.8 %copy-start.5 = (f32[144]{0:T(256)S(1)}, f32[144]{0:T(256)}, u32[]{:S(2)}) copy-start(f32[144]{0:T(256)} %param.12) | copy-start | bytes 1732
  459.8 178.4 %all-reduce.5.cloned.1.call-start = ((), (), s32[]{:S(2)}) async-start(), calls=%async_computation.6 | async-start | bytes 163840 | tf_op jit(solution)/shard_map/psum | solution.py:95
Sparse Core Ops, SparseCore 0:
  10.4 46.5 all-gather.4
  274.0 76.1 reduce-scatter.4
  360.1 44.7 all-gather.6
  410.3 38.0 all-reduce.2
  459.9 80.2 reduce-scatter.6
  542.4 39.0 all-reduce.4
where the time goes:
time: 656 us; the launch traced here: 655 us
  waiting for transfers between devices  273 us (42%)
  local copies, waits for them, and re-layouts  218 us (33%)
  blocking collectives  97.5 us (15%)
  matrix products  37.3 us (6%)
  between operations  15.1 us (2%)
  other arithmetic  13.6 us (2%)
    gather x3, local copies, waits for them, and re-layouts, on_device(): jnp.take(lookup, indices, axis=0)  205 us
    reduce_scatter x1, waiting for transfers between devices, on_device(): lax.psum_scatter(partial_jacobian, 'col', scatter_dimension=2, tiled=True)  76.2 us
    unnamed x7, waiting for transfers between devices  68.2 us
    psum x1, blocking collectives, on_device(): lax.psum(matmul(jacobian_subblock, numerator_sub), ('row', 'col'))  66.1 us
    all_gather x1, waiting for transfers between devices, on_device(): whole_up = lax.all_gather(upstream, 'col', axis=1, tiled=True)  45 us
    all_gather x1, waiting for transfers between devices, on_device(): jac_rows = lax.all_gather(jacobian_subblock, 'col', axis=1, tiled=True)  44.9 us
    psum x1, waiting for transfers between devices, spread(): return lax.psum(block, axis)  38.2 us
    dot_general x15, matrix products, matmul(): return jnp.dot(left, right, precision=FULL_PRECISION)  26.9 us
  transfers between devices with their start and end apart: 6, of which 5 were waited for; matrix products, arithmetic and copies ran while one was open for 4% of the time, Pallas kernels for 0%

commit v1 on v0

v1 whole, which is shorter than its diff:
```python
import functools
import math

import jax
import jax.numpy as jnp
from jax import lax
from jax.experimental import pallas as pl
from jax.experimental.pallas import tpu as pltpu
from jax.sharding import PartitionSpec as P

NS_ITERS = 5
MESH = pl.DeviceIdType.MESH
FULL = lax.Precision.HIGHEST
F32 = jnp.float32
BF16 = jnp.bfloat16
NT = (((1,), (1,)), ((), ()))
TN = (((0,), (0,)), ((), ()))


def gain_kernel(
    rows,
    cols,
    cov_hbm,
    weights_ref,
    act_ref,
    up_ref,
    nb_ref,
    types_ref,
    tgain_ref,
    sens_ref,
    frame_ref,
    noise_ref,
    innov_ref,
    nt_ref,
    g_ref,
    wnew_ref,
    cov_f,
    cov_hi,
    cov_lo,
    nb_all,
    kind_all,
    act_pair,
    sens_pair,
    counts,
    counts_b,
    up_all,
    act_t,
    act_all,
    sens_row,
    sens_all,
    adj_t,
    adj_all,
    w_rows,
    jac_half,
    jac_in,
    jac_piece,
    jac_all,
    n_part,
    n_in,
    n_piece,
    n_col,
    n_slices,
    n_own,
    s_mine,
    s_in,
    cov_sem,
    sib_send,
    sib_recv,
    u_send,
    u_recv,
    a_send,
    a_recv,
    sn_send,
    sn_recv,
    ad_send,
    ad_recv,
    m_send,
    m_recv,
    f_send,
    f_recv,
    y_send,
    y_recv,
    c_send,
    c_recv,
    o_send,
    o_recv,
    s_send,
    s_recv,
):
    r = lax.axis_index("row")
    c = lax.axis_index("col")
    chips = cols // 2
    per = cols // rows
    zs = per // 2
    h = c // 2
    s = c % 2
    x = c // per
    z = (c % per) // 2
    jz = c % per
    other = 1 - s
    sib = c + 1 - 2 * s
    atoms = nb_ref.shape[1]
    pair = 2 * atoms
    nbr = nb_ref.shape[2]
    adjw = up_ref.shape[2]
    actw = act_ref.shape[2]
    mg = sens_ref.shape[0]
    measures = mg * rows
    width = cov_f.shape[1]
    bl = adjw // chips

    def remote(src, dst, ssem, rsem, tr, tc):
        return pltpu.make_async_remote_copy(
            src_ref=src,
            dst_ref=dst,
            send_sem=ssem,
            recv_sem=rsem,
            device_id=(tr, tc),
            device_id_type=MESH,
        )

    cov_in = [
        pltpu.make_async_copy(
            cov_hbm.at[pl.ds(j * width, width)], cov_f.at[j], cov_sem.at[j]
        )
        for j in range(per)
    ]

    sib_copies = [
        remote(nb_ref.at[other], nb_all.at[s], sib_send.at[0], sib_recv.at[0], r, sib),
        remote(act_ref.at[other], act_pair.at[s], sib_send.at[1], sib_recv.at[1], r, sib),
        remote(sens_ref, sens_pair.at[s], sib_send.at[2], sib_recv.at[2], r, sib),
        remote(types_ref.at[other], kind_all.at[s], sib_send.at[3], sib_recv.at[3], r, sib),
    ]
    sib_copies[0].start()
    mine = pl.ds(pl.multiple_of(c * atoms, atoms), atoms)
    own_up = pltpu.make_async_copy(up_ref.at[s], up_all.at[mine], u_recv)
    own_up.start()
    remote(up_ref.at[other], up_all.at[mine], u_send, u_recv, r, sib).start()

    def send_up(k, _):
        to = lax.rem(h + k, chips)
        for f in range(2):
            remote(up_ref.at[f], up_all.at[mine], u_send, u_recv, r, 2 * to + f).start()
        return 0

    lax.fori_loop(1, chips, send_up, 0)
    sib_copies[1].start()
    sib_copies[2].start()
    sib_copies[3].start()
    for copy in cov_in:
        copy.start()

    nb_all[s] = nb_ref[s]
    kind_all[s] = types_ref[s]
    act_pair[s] = act_ref[s]
    sens_pair[s] = sens_ref[...]
    sib_copies[1].wait_recv()
    sib_copies[2].wait_recv()
    act_t[...] = jnp.transpose(
        act_pair[...].reshape(pair, actw).astype(F32)
    ).astype(BF16)
    sens_row[...] = jnp.concatenate([sens_pair[0], sens_pair[1]], axis=1)
    lanes_mine = pl.ds(pl.multiple_of(h * pair, pair), pair)
    own_act = pltpu.make_async_copy(act_t, act_all.at[:, lanes_mine], a_recv)
    own_sens = pltpu.make_async_copy(sens_row, sens_all.at[:, lanes_mine], sn_recv)
    own_act.start()
    own_sens.start()

    def send_act(k, _):
        to = 2 * lax.rem(h + k, chips) + s
        remote(act_t, act_all.at[:, lanes_mine], a_send, a_recv, r, to).start()
        remote(sens_row, sens_all.at[:, lanes_mine], sn_send, sn_recv, r, to).start()
        return 0

    lax.fori_loop(1, chips, send_act, 0)

    sib_copies[0].wait_recv()
    his = counts.shape[0]
    iota_lo = lax.broadcasted_iota(jnp.int32, (128, nbr), 0)
    iota_hi = lax.broadcasted_iota(jnp.int32, (his, nbr), 0)
    unroll = 8

    def count(step, _):
        t = step // (atoms // unroll)
        base = pl.multiple_of(lax.rem(step, atoms // unroll) * unroll, unroll)
        block = nb_all[t, pl.ds(base, unroll), :]
        for u in range(unroll):
            idx = block[u : u + 1, :]
            low = jnp.where((idx & 127) == iota_lo, 1.0, 0.0).astype(BF16)
            high = jnp.where((idx >> 7) == iota_hi, 1.0, 0.0).astype(BF16)
            got = lax.dot_general(high, low, NT, preferred_element_type=F32)
            row = t * atoms + base + u
            counts[:, pl.ds(row, 1), :] = got.reshape(his, 1, 128)
        return 0

    lax.fori_loop(0, pair // unroll, count, 0)
    for k in range(his):
        counts_b[:, k * 128 : (k + 1) * 128] = counts[k].astype(BF16)

    strip = 64

    def split(j):
        def body(i, _):
            at = pl.ds(pl.multiple_of(i * strip, strip), strip)
            value = cov_f[j, at, :]
            high = value.astype(BF16)
            cov_hi[j, at, :] = high
            cov_lo[j, at, :] = (value - high.astype(F32)).astype(BF16)
            return 0

        lax.fori_loop(0, width // strip, body, 0)

    for j in range(per):
        cov_in[j].wait()
        split(j)

    pltpu.make_async_copy(up_all, up_all, u_recv).wait()
    neighbor_sum = jnp.dot(
        counts_b[...], up_all[...], preferred_element_type=F32
    ) * (1.0 / math.sqrt(nbr))
    own = up_all[pl.ds(pl.multiple_of(h * pair, pair), pair), :].astype(F32)
    sib_copies[3].wait_recv()
    kinds = jnp.concatenate([kind_all[0], kind_all[1]], axis=1)
    kinds = jnp.transpose(jnp.broadcast_to(kinds, (adjw, pair)))
    type_scale = jnp.zeros((pair, adjw), F32)
    for kind in range(tgain_ref.shape[0]):
        type_scale = jnp.where(kinds == kind, tgain_ref[kind : kind + 1, :], type_scale)
    adj_t[...] = jnp.transpose(type_scale * (own + neighbor_sum)).reshape(chips, bl, pair)
    own_adj = pltpu.make_async_copy(adj_t.at[h], adj_all.at[:, lanes_mine], ad_recv)
    own_adj.start()

    def send_adj(k, _):
        to = lax.rem(h + k, chips)
        remote(adj_t.at[to], adj_all.at[:, lanes_mine], ad_send, ad_recv, r, 2 * to + s).start()
        return 0

    lax.fori_loop(1, chips, send_adj, 0)

    pltpu.make_async_copy(sens_all, sens_all, sn_recv).wait()
    which = lax.broadcasted_iota(jnp.int32, (mg, 1), 0)
    frame_of = jnp.zeros((mg, 1), jnp.int32)
    for m in range(mg):
        frame_of = jnp.where(which == m, frame_ref[m], frame_of)
    chosen = jnp.where(frame_of == s, 1.0, 0.0).astype(F32)
    sens_all[...] = sens_all[...] * chosen
    pltpu.make_async_copy(act_all, act_all, a_recv).wait()
    pltpu.make_async_copy(adj_all, adj_all, ad_recv).wait()
    for b in range(bl):
        w_rows[mg * b : mg * (b + 1), :] = (sens_all[...] * adj_all[b : b + 1, :]).astype(BF16)
    jac_half[...] = lax.dot_general(
        w_rows[...], act_all[...], NT, preferred_element_type=F32
    ).reshape(2, bl * mg // 2, actw)
    swap = remote(jac_half.at[other], jac_in, sib_send.at[4], sib_recv.at[4], r, sib)
    swap.start()
    swap.wait_recv()
    whole = jac_half[s] + jac_in[...]
    jac_piece[...] = jnp.concatenate(
        [whole[mg * b : mg * (b + 1), :] for b in range(bl // 2)], axis=1
    ).astype(BF16)

    def cast(piece, buf, stage):
        at = pl.ds(pl.multiple_of(mg * r, mg), mg)
        dst = buf.at[jz, at]
        ssem, rsem = m_send.at[stage], m_recv.at[stage, z * rows + r]

        @pl.when(x == r)
        def _():
            pltpu.make_async_copy(piece, dst, rsem).start()

        @pl.when(x != r)
        def _():
            remote(piece, dst, ssem.at[0], rsem, x, c).start()

        def send(k, _):
            to = 2 * lax.rem(h + k, chips) + s
            remote(piece, dst, ssem.at[k], rsem, x, to).start()
            return 0

        lax.fori_loop(1, chips, send, 0)

    def slot(buf, i, core):
        zz = i // rows
        p = lax.rem(i, rows)
        return buf.at[2 * zz + core, pl.ds(pl.multiple_of(mg * p, mg), mg)]

    def relay(buf, stage):
        def step(i, _):
            here = slot(buf, i, s)
            pltpu.make_async_copy(here, here, m_recv.at[stage, i]).wait()
            remote(here, here, f_send.at[stage, i], f_recv.at[stage, i], r, sib).start()
            return 0

        lax.fori_loop(0, chips, step, 0)

    def relayed(buf, stage):
        def step(i, _):
            there = slot(buf, i, other)
            pltpu.make_async_copy(there, there, f_recv.at[stage, i]).wait()
            return 0

        lax.fori_loop(0, chips, step, 0)

    def cast_done(piece, buf, stage):
        @pl.when(x != r)
        def _():
            pltpu.make_async_copy(piece, piece, m_send.at[stage, 0]).wait()

        def step(k, _):
            pltpu.make_async_copy(piece, piece, m_send.at[stage, k]).wait()
            return 0

        lax.fori_loop(1, chips, step, 0)

        def step2(i, _):
            here = slot(buf, i, s)
            pltpu.make_async_copy(here, here, f_send.at[stage, i]).wait()
            return 0

        lax.fori_loop(0, chips, step2, 0)

    cast(jac_piece, jac_all, 0)
    relay(jac_all, 0)

    def times(core):
        def step(zz, _):
            j = 2 * zz + core
            jac = jac_all[j]
            n_part[...] += (
                jnp.dot(jac, cov_hi[j], preferred_element_type=F32)
                + jnp.dot(jac, cov_lo[j], preferred_element_type=F32)
            ).reshape(rows, mg, width)
            return 0

        lax.fori_loop(0, zs, step, 0)

    n_part[...] = jnp.zeros_like(n_part)
    times(s)
    relayed(jac_all, 0)
    times(other)
    for d in range(1, rows):
        to = lax.rem(r + d, rows)
        remote(n_part.at[to], n_in.at[d - 1], y_send.at[d - 1], y_recv.at[d - 1], to, c).start()
    for d in range(1, rows):
        pltpu.make_async_copy(n_in.at[d - 1], n_in.at[d - 1], y_recv.at[d - 1]).wait()
    mine_n = n_part[r]
    for d in range(1, rows):
        mine_n = mine_n + n_in[d - 1]
    n_piece[...] = mine_n.astype(BF16)
    n_col[r] = n_piece[...]
    cast(n_piece, nt_ref, 1)
    for d in range(1, rows):
        to = lax.rem(r + d, rows)
        remote(n_piece, n_col.at[r], c_send.at[d - 1], c_recv.at[d - 1], to, c).start()
    owned = n_slices.shape[2]
    for t in range(width // owned):
        n_slices[t] = mine_n[:, t * owned : (t + 1) * owned]
    for t in range(width // owned):
        to = (width // owned) * jz + t
        here = (x == r) & (to == c)

        @pl.when(here)
        def _():
            pltpu.make_async_copy(n_slices.at[t], n_own.at[r], o_recv.at[r]).start()

        @pl.when(jnp.logical_not(here))
        def _():
            remote(n_slices.at[t], n_own.at[r], o_send.at[t], o_recv.at[r], x, to).start()

    relay(nt_ref, 1)
    relayed(nt_ref, 1)

    def inner(j, acc):
        return acc + lax.dot_general(
            jac_all[j], nt_ref[j], NT, preferred_element_type=F32
        )

    s_mine[...] = lax.fori_loop(0, per, inner, jnp.zeros((measures, measures), F32))
    for d in range(1, rows):
        to = lax.rem(r + d, rows)
        remote(s_mine, s_in.at[d - 1], s_send.at[d - 1], s_recv.at[d - 1], to, c).start()
    for d in range(1, rows):
        pltpu.make_async_copy(s_in.at[d - 1], s_in.at[d - 1], s_recv.at[d - 1]).wait()
    innovation_cov = s_mine[...]
    for d in range(1, rows):
        innovation_cov = innovation_cov + s_in[d - 1]
    i0 = lax.broadcasted_iota(jnp.int32, (measures, measures), 0)
    i1 = lax.broadcasted_iota(jnp.int32, (measures, measures), 1)
    eye = jnp.where(i0 == i1, 1.0, 0.0).astype(F32)
    innovation_cov = innovation_cov + eye * noise_ref[...]
    row_sums = jnp.sum(jnp.abs(innovation_cov), axis=1, keepdims=True)
    first = 1.0 / jnp.max(row_sums, axis=0, keepdims=True)
    inverse = eye * first
    left = eye - innovation_cov * first
    for sweep in range(NS_ITERS):
        inverse = inverse + jnp.dot(inverse, left, precision=FULL, preferred_element_type=F32)
        if sweep < NS_ITERS - 1:
            left = jnp.dot(left, left, precision=FULL, preferred_element_type=F32)
    for d in range(1, rows):
        pltpu.make_async_copy(n_piece, n_piece, c_recv.at[d - 1]).wait()
    n_cols = n_col[...].reshape(measures, width).astype(F32)
    g_ref[...] = jnp.dot(inverse, n_cols, precision=FULL, preferred_element_type=F32).astype(BF16)
    step_col = jnp.sum(inverse * innov_ref[...], axis=1, keepdims=True)
    for p in range(rows):
        pltpu.make_async_copy(n_own.at[p], n_own.at[p], o_recv.at[p]).wait()
    n_mine = n_own[...].reshape(measures, owned)
    wnew_ref[...] = weights_ref[...] + jnp.sum(step_col * n_mine, axis=0, keepdims=True)

    for copy in sib_copies:
        copy.wait_send()
    swap.wait_send()
    sent_up = up_all.at[pl.ds(0, (2 * chips - 1) * atoms)]
    pltpu.make_async_copy(sent_up, sent_up, u_send).wait()
    sent = pl.ds(0, (chips - 1) * pair)
    for buf, sem in ((act_all, a_send), (sens_all, sn_send), (adj_all, ad_send)):
        pltpu.make_async_copy(buf.at[:, sent], buf.at[:, sent], sem).wait()
    cast_done(jac_piece, jac_all, 0)
    cast_done(n_piece, nt_ref, 1)
    for d in range(1, rows):
        pltpu.make_async_copy(n_in.at[0], n_in.at[0], y_send.at[d - 1]).wait()
        pltpu.make_async_copy(n_piece, n_piece, c_send.at[d - 1]).wait()
        pltpu.make_async_copy(s_mine, s_mine, s_send.at[d - 1]).wait()
    for t in range(width // owned):
        to = (width // owned) * jz + t

        @pl.when(jnp.logical_not((x == r) & (to == c)))
        def _():
            pltpu.make_async_copy(n_slices.at[t], n_slices.at[t], o_send.at[t]).wait()


def update_kernel(cov_ref, nt_ref, g_ref, out_ref):
    out_ref[...] = cov_ref[...] - lax.dot_general(
        nt_ref[0], g_ref[...], TN, preferred_element_type=F32
    )


def on_device(
    cov,
    weights,
    act,
    upstream,
    neighbors,
    types,
    type_gain,
    sens,
    frame_for_measure,
    noise_variance,
    innovation,
):
    rows = lax.axis_size("row")
    cols = lax.axis_size("col")
    per = cols // rows
    chips = cols // 2
    frames, atoms, nbr = neighbors.shape
    pair = 2 * atoms
    all_atoms = cols * atoms
    adjw, actw = upstream.shape[2], act.shape[2]
    mg = sens.shape[0]
    measures = mg * rows
    width = cov.shape[1]
    owned = weights.shape[0]
    bl = adjw // chips
    his = all_atoms // 128
    dma = pltpu.SemaphoreType.DMA
    vmem = pl.BlockSpec(memory_space=pltpu.VMEM)
    n_rows, gain, weights_new = pl.pallas_call(
        functools.partial(gain_kernel, rows, cols),
        out_shape=(
            jax.ShapeDtypeStruct((per, measures, width), BF16),
            jax.ShapeDtypeStruct((measures, width), BF16),
            jax.ShapeDtypeStruct((1, owned), F32),
        ),
        in_specs=[pl.BlockSpec(memory_space=pl.ANY)]
        + [vmem] * 7
        + [pl.BlockSpec(memory_space=pltpu.SMEM)]
        + [vmem] * 2,
        out_specs=(vmem,) * 3,
        scratch_shapes=[
            pltpu.VMEM((per, width, width), F32),
            pltpu.VMEM((per, width, width), BF16),
            pltpu.VMEM((per, width, width), BF16),
            pltpu.VMEM((2, atoms, nbr), jnp.int32),
            pltpu.VMEM((2, 1, atoms), jnp.int32),
            pltpu.VMEM((2, atoms, actw), BF16),
            pltpu.VMEM((2, mg, atoms), F32),
            pltpu.VMEM((his, pair, 128), F32),
            pltpu.VMEM((pair, all_atoms), BF16),
            pltpu.VMEM((all_atoms, adjw), BF16),
            pltpu.VMEM((actw, pair), BF16),
            pltpu.VMEM((actw, all_atoms), BF16),
            pltpu.VMEM((mg, pair), F32),
            pltpu.VMEM((mg, all_atoms), F32),
            pltpu.VMEM((chips, bl, pair), F32),
            pltpu.VMEM((bl, all_atoms), F32),
            pltpu.VMEM((bl * mg, all_atoms), BF16),
            pltpu.VMEM((2, bl * mg // 2, actw), F32),
            pltpu.VMEM((bl * mg // 2, actw), F32),
            pltpu.VMEM((mg, width), BF16),
            pltpu.VMEM((per, measures, width), BF16),
            pltpu.VMEM((rows, mg, width), F32),
            pltpu.VMEM((rows - 1, mg, width), F32),
            pltpu.VMEM((mg, width), BF16),
            pltpu.VMEM((rows, mg, width), BF16),
            pltpu.VMEM((width // owned, mg, owned), F32),
            pltpu.VMEM((rows, mg, owned), F32),
            pltpu.VMEM((measures, measures), F32),
            pltpu.VMEM((rows - 1, measures, measures), F32),
            dma((per,)),
            dma((5,)),
            dma((5,)),
            dma,
            dma,
            dma,
            dma,
            dma,
            dma,
            dma,
            dma,
            dma((2, chips)),
            dma((2, chips)),
            dma((2, chips)),
            dma((2, chips)),
            dma((rows - 1,)),
            dma((rows - 1,)),
            dma((rows - 1,)),
            dma((rows - 1,)),
            dma((width // owned,)),
            dma((rows,)),
            dma((rows - 1,)),
            dma((rows - 1,)),
        ],
        compiler_params=pltpu.CompilerParams(
            has_side_effects=True, vmem_limit_bytes=52 * 2**20
        ),
        name="gain",
    )(
        cov,
        weights.reshape(1, owned),
        act,
        upstream,
        neighbors,
        types.reshape(frames, 1, atoms),
        type_gain,
        sens,
        frame_for_measure,
        noise_variance.reshape(1, measures),
        innovation.reshape(1, measures),
    )
    cov_new = pl.pallas_call(
        update_kernel,
        grid=(per,),
        in_specs=[
            pl.BlockSpec((width, width), lambda j: (j, 0)),
            pl.BlockSpec((1, measures, width), lambda j: (j, 0, 0)),
            pl.BlockSpec((measures, width), lambda j: (0, 0)),
        ],
        out_specs=pl.BlockSpec((width, width), lambda j: (j, 0)),
        out_shape=jax.ShapeDtypeStruct(cov.shape, F32),
        compiler_params=pltpu.CompilerParams(vmem_limit_bytes=32 * 2**20),
        name="update",
    )(cov, n_rows, gain)
    return weights_new.reshape(owned), cov_new


def solution(mesh):
    return jax.shard_map(
        on_device,
        mesh=mesh,
        in_specs=(
            P("row", "col"),
            P(("row", "col")),
            P("row", "col", None),
            P("row", "col", None),
            P("row", "col", None),
            P("row", "col"),
            P(),
            P("row", "col"),
            P("row"),
            P(),
            P(),
        ),
        out_specs=(P(("row", "col")), P("row", "col")),
        check_vma=False,
    )
```

time: 656 us -> 109 us (0.17)
  waiting for transfers between devices: 273 us -> 0 us
  local copies, waits for them, and re-layouts: 218 us -> 29.3 us
  blocking collectives: 97.5 us -> 0 us
  Pallas kernels: 0 us -> 78.6 us
  matrix products: 37.3 us -> 0 us
  between operations: 15.1 us -> 0.8 us
  other arithmetic: 13.6 us -> 0 us
    gather x5 -> x0, local copies, waits for them, and re-layouts: 206 us -> none  [the longest x3 205 us: on_device(): jnp.take(lookup, indices, axis=0)]
    all_gather x2 -> x0, waiting for transfers between devices: 89.9 us -> none  [the longest x1 45 us: on_device(): whole_up = lax.all_gather(upstream, 'col', axis=1, tiled=True)]
    pallas_call x0 -> x2, Pallas kernels: none -> 78.6 us  [the longest x1 70.7 us: on_device(): pl.pallas_call(functools.partial(gain_kernel, rows, cols), out_shape=(jax...]
    reduce_scatter x1 -> x0, waiting for transfers between devices: 76.2 us -> none  [on_device(): lax.psum_scatter(partial_jacobian, 'col', scatter_dimension=2, tiled=True)]
    unnamed x7 -> x0, waiting for transfers between devices: 68.2 us -> none
    psum x1 -> x0, blocking collectives: 66.1 us -> none  [on_device(): lax.psum(matmul(jacobian_subblock, numerator_sub), ('row', 'col'))]
    psum x2 -> x0, waiting for transfers between devices: 38.2 us -> none  [the longest x1 38.2 us: spread(): return lax.psum(block, axis)]
    dot_general x18 -> x0, matrix products: 37.3 us -> none  [the longest x15 26.9 us: matmul(): return jnp.dot(left, right, precision=FULL_PRECISION)]
  transfers between devices with their start and end apart: 6 -> 0, of which waited for: 5 -> 0; matrix products, arithmetic and copies ran while one was open for 4% -> 0% of each run, Pallas kernels for 0% -> 0%
where the time goes in v1:
time: 109 us
  Pallas kernels  78.6 us (72%)
  local copies, waits for them, and re-layouts  29.3 us (27%)
    pallas_call x1, Pallas kernels, on_device(): pl.pallas_call(functools.partial(gain_kernel, rows, cols), out_shape=(jax...  70.7 us
    unnamed x25, local copies, waits for them, and re-layouts  29.3 us
    pallas_call x1, Pallas kernels, on_device(): pl.pallas_call(update_kernel, grid=(per,), in_specs=[pl.BlockSpec((width,...  7.86 us

profile of v1, /device:TPU:1, one launch (start us, length us, event | category | flops | bytes accessed | tf_op | source)
XLA Modules:
  0.0 108.7 jit_solution(15851031038929914832)
XLA Ops:
  0.6 0.0 copy-start.10
  0.6 0.0 copy-start.9
  0.7 0.0 copy-start.8
  0.7 0.0 copy-start.4
  0.7 0.0 copy-start.7
  0.7 0.0 copy-start.6
  0.7 0.0 copy-start.1
  0.7 0.0 copy-start.3
  0.7 0.0 copy-start.2
  0.7 0.0 copy-start.5
  0.7 12.2 %copy.13.cov_hbm.cov_ref = f32[4608,576]{1,0:T(8,128)} copy(f32[4608,576]{0,1:T(8,128)} %param.11) | data formatting | bytes 21233664 | tf_op args[0]
  12.9 0.0 copy-done.10
  12.9 0.0 copy-done.9
  12.9 0.0 copy-done.8
  12.9 0.0 copy-done.4
  13.0 0.0 copy-done.7
  13.0 0.0 copy-done.6
  13.0 0.0 copy-done.1
  13.0 0.0 copy-done.3
  13.0 0.0 copy-done.2
  13.0 0.0 copy-done.5
  13.0 70.7 %gain.1 = (bf16[8,64,576]{2,1,0:T(8,128)(2,1)S(1)}, bf16[64,576]{1,0:T(8,128)(2,1)S(1)}, f32[1,144]{1,0:T(1,128)S(1)}) custom-call(f32[4608,576]{1,0:T(8,128)} %copy.13.cov_hbm.cov_ref, f32[1,144]{1,0:T(1,128)S(1)} %bitcast.7, bf16[2,64,144]{2,1,0:T(8,128)(2,1)S(1)} %copy-done.2, bf16[2,64,128]{2,1,0:T(8,128)(2,1)S(1)} %copy-done.3, ...), custom_call_target="tpu_custom_call" | custom-call | tf_op jit(solution)/shard_map/gain/pallas_call | solution.py:466
  83.8 7.9 %update.1 = f32[4608,576]{1,0:T(8,128)S(1)} custom-call(f32[4608,576]{1,0:T(8,128)} %copy.13.cov_hbm.cov_ref, bf16[8,64,576]{2,1,0:T(8,128)(2,1)S(1)} %get-tuple-element.6.nt_ref, bf16[64,576]{1,0:T(8,128)(2,1)S(1)} %get-tuple-element.7.g_ref), custom_call_target="tpu_custom_call" | custom-call | tf_op jit(solution)/shard_map/update/pallas_call | solution.py:549
  91.6 0.0 copy-start
  91.6 4.4 %copy-done = f32[4608,576]{1,0:T(8,128)} copy-done((f32[4608,576]{1,0:T(8,128)}, f32[4608,576]{1,0:T(8,128)S(1)}, u32[]{:S(2)}) %copy-start) | copy-done | bytes 10616856
  96.0 12.1 %copy.16 = f32[4608,576]{0,1:T(8,128)} copy(f32[4608,576]{1,0:T(8,128)} %copy-done) | data formatting | bytes 21233664
  108.1 0.6 copy.18
Async XLA Ops:
  0.6 12.3 %copy-start.10 = (f32[64]{0:T(128)S(1)}, f32[64]{0:T(128)}, u32[]{:S(2)}) copy-start(f32[64]{0:T(128)} %param.21) | copy-start | bytes 772
  0.6 12.3 %copy-start.9 = (f32[64]{0:T(128)S(1)}, f32[64]{0:T(128)}, u32[]{:S(2)}) copy-start(f32[64]{0:T(128)} %param.20) | copy-start | bytes 772
  0.7 12.3 %copy-start.8 = (s32[16]{0:T(128)S(1)}, s32[16]{0:T(128)}, u32[]{:S(2)}) copy-start(s32[16]{0:T(128)} %frame_ref.1) | copy-start | bytes 196
  0.7 12.3 %copy-start.4 = (f32[16,64]{1,0:T(8,128)S(1)}, f32[16,64]{1,0:T(8,128)}, u32[]{:S(2)}) copy-start(f32[16,64]{1,0:T(8,128)} %sens_ref.1) | copy-start | bytes 12292
  0.7 12.3 %copy-start.7 = (f32[2,128]{1,0:T(2,128)S(1)}, f32[2,128]{1,0:T(2,128)}, u32[]{:S(2)}) copy-start(f32[2,128]{1,0:T(2,128)} %tgain_ref.1) | copy-start | bytes 3076
  0.7 12.3 %copy-start.6 = (s32[2,64]{1,0:T(2,128)S(1)}, s32[2,64]{1,0:T(2,128)}, u32[]{:S(2)}) copy-start(s32[2,64]{1,0:T(2,128)} %param.16) | copy-start | bytes 1540
  0.7 12.3 %copy-start.1 = (s32[2,64,138]{2,1,0:T(8,128)S(1)}, s32[2,64,138]{2,1,0:T(8,128)}, u32[]{:S(2)}) copy-start(s32[2,64,138]{2,1,0:T(8,128)} %nb_ref.1) | copy-start | bytes 211972
  0.7 12.3 %copy-start.3 = (bf16[2,64,128]{2,1,0:T(8,128)(2,1)S(1)}, bf16[2,64,128]{2,1,0:T(8,128)(2,1)}, u32[]{:S(2)}) copy-start(bf16[2,64,128]{2,1,0:T(8,128)(2,1)} %up_ref.1) | copy-start | bytes 98308
  0.7 12.3 %copy-start.2 = (bf16[2,64,144]{2,1,0:T(8,128)(2,1)S(1)}, bf16[2,64,144]{2,1,0:T(8,128)(2,1)}, u32[]{:S(2)}) copy-start(bf16[2,64,144]{2,1,0:T(8,128)(2,1)} %act_ref.1) | copy-start | bytes 110596
  0.7 12.3 %copy-start.5 = (f32[144]{0:T(256)S(1)}, f32[144]{0:T(256)}, u32[]{:S(2)}) copy-start(f32[144]{0:T(256)} %param.12) | copy-start | bytes 1732
  91.6 4.4 %copy-start = (f32[4608,576]{1,0:T(8,128)}, f32[4608,576]{1,0:T(8,128)S(1)}, u32[]{:S(2)}) copy-start(f32[4608,576]{1,0:T(8,128)S(1)} %update.1) | copy-start | bytes 31850500

commit v2 on v1

--- a/solution.py
+++ b/solution.py
@@ -14,7 +14,6 @@
 F32 = jnp.float32
 BF16 = jnp.bfloat16
 NT = (((1,), (1,)), ((), ()))
-TN = (((0,), (0,)), ((), ()))
 
 
 def gain_kernel(
@@ -32,7 +31,7 @@
     noise_ref,
     innov_ref,
     nt_ref,
-    g_ref,
+    gt_ref,
     wnew_ref,
     cov_f,
     cov_hi,
@@ -58,6 +57,8 @@
     n_part,
     n_in,
     n_piece,
+    n_pair,
+    n_wide,
     n_col,
     n_slices,
     n_own,
@@ -97,6 +98,8 @@
     x = c // per
     z = (c % per) // 2
     jz = c % per
+    parity = lax.rem(h + s, 2)
+    drains = []
     other = 1 - s
     sib = c + 1 - 2 * s
     atoms = nb_ref.shape[1]
@@ -106,7 +109,7 @@
     actw = act_ref.shape[2]
     mg = sens_ref.shape[0]
     measures = mg * rows
-    width = cov_f.shape[1]
+    width, chunk = cov_f.shape[1:]
     bl = adjw // chips
 
     def remote(src, dst, ssem, rsem, tr, tc):
@@ -121,9 +124,9 @@
 
     cov_in = [
         pltpu.make_async_copy(
-            cov_hbm.at[pl.ds(j * width, width)], cov_f.at[j], cov_sem.at[j]
+            cov_hbm.at[:, pl.ds(j * chunk, chunk)], cov_f.at[j], cov_sem.at[j]
         )
-        for j in range(per)
+        for j in range(zs)
     ]
 
     sib_copies = [
@@ -175,6 +178,17 @@
 
     lax.fori_loop(1, chips, send_act, 0)
 
+    def drain_first():
+        for copy in sib_copies:
+            copy.wait_send()
+        sent_up = up_all.at[pl.ds(0, (2 * chips - 1) * atoms)]
+        pltpu.make_async_copy(sent_up, sent_up, u_send).wait()
+        for buf, sem in ((act_all, a_send), (sens_all, sn_send)):
+            part = buf.at[:, pl.ds(0, (chips - 1) * pair)]
+            pltpu.make_async_copy(part, part, sem).wait()
+
+    drains.append(drain_first)
+
     sib_copies[0].wait_recv()
     his = counts.shape[0]
     iota_lo = lax.broadcasted_iota(jnp.int32, (128, nbr), 0)
@@ -211,7 +225,7 @@
 
         lax.fori_loop(0, width // strip, body, 0)
 
-    for j in range(per):
+    for j in range(zs):
         cov_in[j].wait()
         split(j)
 
@@ -237,6 +251,12 @@
 
     lax.fori_loop(1, chips, send_adj, 0)
 
+    def drain_adj():
+        part = adj_all.at[:, pl.ds(0, (chips - 1) * pair)]
+        pltpu.make_async_copy(part, part, ad_send).wait()
+
+    drains.append(drain_adj)
+
     pltpu.make_async_copy(sens_all, sens_all, sn_recv).wait()
     which = lax.broadcasted_iota(jnp.int32, (mg, 1), 0)
     frame_of = jnp.zeros((mg, 1), jnp.int32)
@@ -250,113 +270,137 @@
         w_rows[mg * b : mg * (b + 1), :] = (sens_all[...] * adj_all[b : b + 1, :]).astype(BF16)
     jac_half[...] = lax.dot_general(
         w_rows[...], act_all[...], NT, preferred_element_type=F32
-    ).reshape(2, bl * mg // 2, actw)
-    swap = remote(jac_half.at[other], jac_in, sib_send.at[4], sib_recv.at[4], r, sib)
+    )
+    swap = remote(jac_half, jac_in, sib_send.at[4], sib_recv.at[4], r, sib)
     swap.start()
     swap.wait_recv()
-    whole = jac_half[s] + jac_in[...]
+    whole = jac_half[...] + jac_in[...]
     jac_piece[...] = jnp.concatenate(
-        [whole[mg * b : mg * (b + 1), :] for b in range(bl // 2)], axis=1
+        [whole[mg * b : mg * (b + 1), :] for b in range(bl)], axis=1
     ).astype(BF16)
+    drains.append(swap.wait_send)
+
+    half = chips // 2
 
     def cast(piece, buf, stage):
         at = pl.ds(pl.multiple_of(mg * r, mg), mg)
-        dst = buf.at[jz, at]
-        ssem, rsem = m_send.at[stage], m_recv.at[stage, z * rows + r]
-
-        @pl.when(x == r)
+        lanes = pl.ds(pl.multiple_of(chunk * z, chunk), chunk)
+        dst = buf.at[at, lanes]
+        rsem = m_recv.at[stage, z * rows + r]
+        own = (x == r) & (s == 0)
+
+        @pl.when(own)
         def _():
             pltpu.make_async_copy(piece, dst, rsem).start()
 
-        @pl.when(x != r)
+        @pl.when(jnp.logical_not(own))
         def _():
-            remote(piece, dst, ssem.at[0], rsem, x, c).start()
-
-        def send(k, _):
-            to = 2 * lax.rem(h + k, chips) + s
-            remote(piece, dst, ssem.at[k], rsem, x, to).start()
+            to = 2 * lax.rem(h + s, chips) + s
+            remote(piece, dst, m_send.at[stage, 0], rsem, x, to).start()
+
+        def send(i, _):
+            to = 2 * lax.rem(h + 2 * i + s, chips) + s
+            remote(piece, dst, m_send.at[stage, i], rsem, x, to).start()
             return 0
 
-        lax.fori_loop(1, chips, send, 0)
-
-    def slot(buf, i, core):
-        zz = i // rows
+        lax.fori_loop(1, half, send, 0)
+
+        def drain():
+            @pl.when(jnp.logical_not(own))
+            def _():
+                pltpu.make_async_copy(piece, piece, m_send.at[stage, 0]).wait()
+
+            def step(i, _):
+                pltpu.make_async_copy(piece, piece, m_send.at[stage, i]).wait()
+                return 0
+
+            lax.fori_loop(1, half, step, 0)
+
+        drains.append(drain)
+
+    def slot(buf, i, which):
+        zz = 2 * (i // rows) + which
         p = lax.rem(i, rows)
-        return buf.at[2 * zz + core, pl.ds(pl.multiple_of(mg * p, mg), mg)]
+        lanes = pl.ds(pl.multiple_of(chunk * zz, chunk), chunk)
+        return buf.at[pl.ds(pl.multiple_of(mg * p, mg), mg), lanes], zz * rows + p
 
     def relay(buf, stage):
         def step(i, _):
-            here = slot(buf, i, s)
-            pltpu.make_async_copy(here, here, m_recv.at[stage, i]).wait()
-            remote(here, here, f_send.at[stage, i], f_recv.at[stage, i], r, sib).start()
+            here, k = slot(buf, i, parity)
+            pltpu.make_async_copy(here, here, m_recv.at[stage, k]).wait()
+            remote(here, here, f_send.at[stage, i], f_recv.at[stage, k], r, sib).start()
             return 0
 
-        lax.fori_loop(0, chips, step, 0)
+        lax.fori_loop(0, half, step, 0)
+
+        def drain():
+            def step2(i, _):
+                here, _ = slot(buf, i, parity)
+                pltpu.make_async_copy(here, here, f_send.at[stage, i]).wait()
+                return 0
+
+            lax.fori_loop(0, half, step2, 0)
+
+        drains.append(drain)
 
     def relayed(buf, stage):
         def step(i, _):
-            there = slot(buf, i, other)
-            pltpu.make_async_copy(there, there, f_recv.at[stage, i]).wait()
+            there, k = slot(buf, i, 1 - parity)
+            pltpu.make_async_copy(there, there, f_recv.at[stage, k]).wait()
             return 0
 
-        lax.fori_loop(0, chips, step, 0)
-
-    def cast_done(piece, buf, stage):
-        @pl.when(x != r)
-        def _():
-            pltpu.make_async_copy(piece, piece, m_send.at[stage, 0]).wait()
-
-        def step(k, _):
-            pltpu.make_async_copy(piece, piece, m_send.at[stage, k]).wait()
-            return 0
-
-        lax.fori_loop(1, chips, step, 0)
-
-        def step2(i, _):
-            here = slot(buf, i, s)
-            pltpu.make_async_copy(here, here, f_send.at[stage, i]).wait()
-            return 0
-
-        lax.fori_loop(0, chips, step2, 0)
+        lax.fori_loop(0, half, step, 0)
 
     cast(jac_piece, jac_all, 0)
     relay(jac_all, 0)
 
-    def times(core):
-        def step(zz, _):
-            j = 2 * zz + core
-            jac = jac_all[j]
+    def times(which):
+        def step(i, _):
+            zz = 2 * i + which
+            jac = jac_all[:, pl.ds(pl.multiple_of(chunk * zz, chunk), chunk)]
             n_part[...] += (
-                jnp.dot(jac, cov_hi[j], preferred_element_type=F32)
-                + jnp.dot(jac, cov_lo[j], preferred_element_type=F32)
+                lax.dot_general(jac, cov_hi[zz], NT, preferred_element_type=F32)
+                + lax.dot_general(jac, cov_lo[zz], NT, preferred_element_type=F32)
             ).reshape(rows, mg, width)
             return 0
 
-        lax.fori_loop(0, zs, step, 0)
+        lax.fori_loop(0, zs // 2, step, 0)
 
     n_part[...] = jnp.zeros_like(n_part)
-    times(s)
+    times(parity)
     relayed(jac_all, 0)
-    times(other)
+    times(1 - parity)
     for d in range(1, rows):
         to = lax.rem(r + d, rows)
-        remote(n_part.at[to], n_in.at[d - 1], y_send.at[d - 1], y_recv.at[d - 1], to, c).start()
+        copy = remote(n_part.at[to], n_in.at[d - 1], y_send.at[d - 1], y_recv.at[d - 1], to, c)
+        copy.start()
+        drains.append(copy.wait_send)
     for d in range(1, rows):
         pltpu.make_async_copy(n_in.at[d - 1], n_in.at[d - 1], y_recv.at[d - 1]).wait()
     mine_n = n_part[r]
     for d in range(1, rows):
         mine_n = mine_n + n_in[d - 1]
     n_piece[...] = mine_n.astype(BF16)
+    swap_n = remote(n_piece, n_pair.at[s], sib_send.at[5], sib_recv.at[5], r, sib)
+    swap_n.start()
+    drains.append(swap_n.wait_send)
+    n_pair[s] = n_piece[...]
     n_col[r] = n_piece[...]
-    cast(n_piece, nt_ref, 1)
     for d in range(1, rows):
         to = lax.rem(r + d, rows)
-        remote(n_piece, n_col.at[r], c_send.at[d - 1], c_recv.at[d - 1], to, c).start()
+        copy = remote(n_piece, n_col.at[r], c_send.at[d - 1], c_recv.at[d - 1], to, c)
+        copy.start()
+        drains.append(copy.wait_send)
+    swap_n.wait_recv()
+    n_wide[...] = jnp.concatenate(
+        [n_pair[0].astype(F32), n_pair[1].astype(F32)], axis=1
+    ).astype(BF16)
+    cast(n_wide, nt_ref, 1)
     owned = n_slices.shape[2]
-    for t in range(width // owned):
+    for t in range(rows):
         n_slices[t] = mine_n[:, t * owned : (t + 1) * owned]
-    for t in range(width // owned):
-        to = (width // owned) * jz + t
+    for t in range(rows):
+        to = rows * jz + t
         here = (x == r) & (to == c)
 
         @pl.when(here)
@@ -370,15 +414,14 @@
     relay(nt_ref, 1)
     relayed(nt_ref, 1)
 
-    def inner(j, acc):
-        return acc + lax.dot_general(
-            jac_all[j], nt_ref[j], NT, preferred_element_type=F32
-        )
-
-    s_mine[...] = lax.fori_loop(0, per, inner, jnp.zeros((measures, measures), F32))
+    s_mine[...] = lax.dot_general(
+        jac_all[...], nt_ref[...], NT, preferred_element_type=F32
+    )
     for d in range(1, rows):
         to = lax.rem(r + d, rows)
-        remote(s_mine, s_in.at[d - 1], s_send.at[d - 1], s_recv.at[d - 1], to, c).start()
+        copy = remote(s_mine, s_in.at[d - 1], s_send.at[d - 1], s_recv.at[d - 1], to, c)
+        copy.start()
+        drains.append(copy.wait_send)
     for d in range(1, rows):
         pltpu.make_async_copy(s_in.at[d - 1], s_in.at[d - 1], s_recv.at[d - 1]).wait()
     innovation_cov = s_mine[...]
@@ -399,38 +442,28 @@
     for d in range(1, rows):
         pltpu.make_async_copy(n_piece, n_piece, c_recv.at[d - 1]).wait()
     n_cols = n_col[...].reshape(measures, width).astype(F32)
-    g_ref[...] = jnp.dot(inverse, n_cols, precision=FULL, preferred_element_type=F32).astype(BF16)
+    gt_ref[...] = jnp.transpose(
+        jnp.dot(inverse, n_cols, precision=FULL, preferred_element_type=F32)
+    ).astype(BF16)
     step_col = jnp.sum(inverse * innov_ref[...], axis=1, keepdims=True)
     for p in range(rows):
         pltpu.make_async_copy(n_own.at[p], n_own.at[p], o_recv.at[p]).wait()
     n_mine = n_own[...].reshape(measures, owned)
     wnew_ref[...] = weights_ref[...] + jnp.sum(step_col * n_mine, axis=0, keepdims=True)
-
-    for copy in sib_copies:
-        copy.wait_send()
-    swap.wait_send()
-    sent_up = up_all.at[pl.ds(0, (2 * chips - 1) * atoms)]
-    pltpu.make_async_copy(sent_up, sent_up, u_send).wait()
-    sent = pl.ds(0, (chips - 1) * pair)
-    for buf, sem in ((act_all, a_send), (sens_all, sn_send), (adj_all, ad_send)):
-        pltpu.make_async_copy(buf.at[:, sent], buf.at[:, sent], sem).wait()
-    cast_done(jac_piece, jac_all, 0)
-    cast_done(n_piece, nt_ref, 1)
-    for d in range(1, rows):
-        pltpu.make_async_copy(n_in.at[0], n_in.at[0], y_send.at[d - 1]).wait()
-        pltpu.make_async_copy(n_piece, n_piece, c_send.at[d - 1]).wait()
-        pltpu.make_async_copy(s_mine, s_mine, s_send.at[d - 1]).wait()
-    for t in range(width // owned):
-        to = (width // owned) * jz + t
+    for t in range(rows):
+        to = rows * jz + t
 
         @pl.when(jnp.logical_not((x == r) & (to == c)))
         def _():
             pltpu.make_async_copy(n_slices.at[t], n_slices.at[t], o_send.at[t]).wait()
 
-
-def update_kernel(cov_ref, nt_ref, g_ref, out_ref):
-    out_ref[...] = cov_ref[...] - lax.dot_general(
-        nt_ref[0], g_ref[...], TN, preferred_element_type=F32
+    for drain in drains:
+        drain()
+
+
+def update_kernel(cov_ref, nt_ref, gt_ref, out_ref):
+    out_ref[...] = cov_ref[...] - jnp.dot(
+        gt_ref[...], nt_ref[...], preferred_element_type=F32
     )
 
 
@@ -457,17 +490,20 @@
     adjw, actw = upstream.shape[2], act.shape[2]
     mg = sens.shape[0]
     measures = mg * rows
-    width = cov.shape[1]
+    height, width = cov.shape
+    zs = per // 2
+    chunk = height // zs
     owned = weights.shape[0]
     bl = adjw // chips
     his = all_atoms // 128
     dma = pltpu.SemaphoreType.DMA
     vmem = pl.BlockSpec(memory_space=pltpu.VMEM)
+    covariance = cov.T
     n_rows, gain, weights_new = pl.pallas_call(
         functools.partial(gain_kernel, rows, cols),
         out_shape=(
-            jax.ShapeDtypeStruct((per, measures, width), BF16),
-            jax.ShapeDtypeStruct((measures, width), BF16),
+            jax.ShapeDtypeStruct((measures, height), BF16),
+            jax.ShapeDtypeStruct((width, measures), BF16),
             jax.ShapeDtypeStruct((1, owned), F32),
         ),
         in_specs=[pl.BlockSpec(memory_space=pl.ANY)]
@@ -476,9 +512,9 @@
         + [vmem] * 2,
         out_specs=(vmem,) * 3,
         scratch_shapes=[
-            pltpu.VMEM((per, width, width), F32),
-            pltpu.VMEM((per, width, width), BF16),
-            pltpu.VMEM((per, width, width), BF16),
+            pltpu.VMEM((zs, width, chunk), F32),
+            pltpu.VMEM((zs, width, chunk), BF16),
+            pltpu.VMEM((zs, width, chunk), BF16),
             pltpu.VMEM((2, atoms, nbr), jnp.int32),
             pltpu.VMEM((2, 1, atoms), jnp.int32),
             pltpu.VMEM((2, atoms, actw), BF16),
@@ -493,38 +529,40 @@
             pltpu.VMEM((chips, bl, pair), F32),
             pltpu.VMEM((bl, all_atoms), F32),
             pltpu.VMEM((bl * mg, all_atoms), BF16),
-            pltpu.VMEM((2, bl * mg // 2, actw), F32),
-            pltpu.VMEM((bl * mg // 2, actw), F32),
-            pltpu.VMEM((mg, width), BF16),
-            pltpu.VMEM((per, measures, width), BF16),
+            pltpu.VMEM((bl * mg, actw), F32),
+            pltpu.VMEM((bl * mg, actw), F32),
+            pltpu.VMEM((mg, chunk), BF16),
+            pltpu.VMEM((measures, height), BF16),
             pltpu.VMEM((rows, mg, width), F32),
             pltpu.VMEM((rows - 1, mg, width), F32),
             pltpu.VMEM((mg, width), BF16),
+            pltpu.VMEM((2, mg, width), BF16),
+            pltpu.VMEM((mg, chunk), BF16),
             pltpu.VMEM((rows, mg, width), BF16),
-            pltpu.VMEM((width // owned, mg, owned), F32),
+            pltpu.VMEM((rows, mg, owned), F32),
             pltpu.VMEM((rows, mg, owned), F32),
             pltpu.VMEM((measures, measures), F32),
             pltpu.VMEM((rows - 1, measures, measures), F32),
-            dma((per,)),
-            dma((5,)),
-            dma((5,)),
-            dma,
-            dma,
-            dma,
-            dma,
-            dma,
-            dma,
-            dma,
-            dma,
-            dma((2, chips)),
-            dma((2, chips)),
-            dma((2, chips)),
-            dma((2, chips)),
+            dma((zs,)),
+            dma((6,)),
+            dma((6,)),
+            dma,
+            dma,
+            dma,
+            dma,
+            dma,
+            dma,
+            dma,
+            dma,
+            dma((2, chips // 2)),
+            dma((2, zs * rows)),
+            dma((2, chips // 2)),
+            dma((2, zs * rows)),
             dma((rows - 1,)),
             dma((rows - 1,)),
             dma((rows - 1,)),
             dma((rows - 1,)),
-            dma((width // owned,)),
+            dma((rows,)),
             dma((rows,)),
             dma((rows - 1,)),
             dma((rows - 1,)),
@@ -534,7 +572,7 @@
         ),
         name="gain",
     )(
-        cov,
+        covariance,
         weights.reshape(1, owned),
         act,
         upstream,
@@ -546,20 +584,21 @@
         noise_variance.reshape(1, measures),
         innovation.reshape(1, measures),
     )
+    tile = width // per
     cov_new = pl.pallas_call(
         update_kernel,
         grid=(per,),
         in_specs=[
-            pl.BlockSpec((width, width), lambda j: (j, 0)),
-            pl.BlockSpec((1, measures, width), lambda j: (j, 0, 0)),
-            pl.BlockSpec((measures, width), lambda j: (0, 0)),
+            pl.BlockSpec((tile, height), lambda j: (j, 0)),
+            pl.BlockSpec((measures, height), lambda j: (0, 0)),
+            pl.BlockSpec((tile, measures), lambda j: (j, 0)),
         ],
-        out_specs=pl.BlockSpec((width, width), lambda j: (j, 0)),
-        out_shape=jax.ShapeDtypeStruct(cov.shape, F32),
+        out_specs=pl.BlockSpec((tile, height), lambda j: (j, 0)),
+        out_shape=jax.ShapeDtypeStruct((width, height), F32),
         compiler_params=pltpu.CompilerParams(vmem_limit_bytes=32 * 2**20),
         name="update",
-    )(cov, n_rows, gain)
-    return weights_new.reshape(owned), cov_new
+    )(covariance, n_rows, gain)
+    return weights_new.reshape(owned), cov_new.T
 
 
 def solution(mesh):

time: 109 us -> 85.1 us (0.78)
  local copies, waits for them, and re-layouts: 29.3 us -> 8.44 us
  Pallas kernels: 78.6 us -> 75.6 us
    unnamed x25 -> x23, local copies, waits for them, and re-layouts: 29.3 us -> 8.44 us
    pallas_call x1, Pallas kernels: 7.86 us -> 6.02 us  [on_device(): pl.pallas_call(update_kernel, grid=(per,), in_specs=[pl.BlockSpec((tile,...]
    pallas_call x1, Pallas kernels: 70.7 us -> 69.5 us  [on_device(): pl.pallas_call(functools.partial(gain_kernel, rows, cols), out_shape=(jax...]
where the time goes in v2:
time: 85.1 us; the launch traced here: 84.7 us
  Pallas kernels  75.6 us (89%)
  local copies, waits for them, and re-layouts  8.44 us (10%)
    pallas_call x1, Pallas kernels, on_device(): pl.pallas_call(functools.partial(gain_kernel, rows, cols), out_shape=(jax...  69.5 us
    unnamed x23, local copies, waits for them, and re-layouts  8.44 us
    pallas_call x1, Pallas kernels, on_device(): pl.pallas_call(update_kernel, grid=(per,), in_specs=[pl.BlockSpec((tile,...  6.02 us

profile of v2, /device:TPU:1, one launch (start us, length us, event | category | flops | bytes accessed | tf_op | source)
XLA Modules:
  0.0 84.7 jit_solution(10198816508352614654)
XLA Ops:
  0.6 0.0 copy-start
  0.6 0.0 copy-start.1
  0.7 1.0 %copy-done.1 = s32[2,64,138]{2,1,0:T(8,128)S(1)} copy-done((s32[2,64,138]{2,1,0:T(8,128)S(1)}, s32[2,64,138]{2,1,0:T(8,128)}, u32[]{:S(2)}) %copy-start.1) | copy-done | bytes 70680
  1.7 0.0 copy-start.2
  1.7 1.0 %copy-done.2 = bf16[2,64,144]{2,1,0:T(8,128)(2,1)S(1)} copy-done((bf16[2,64,144]{2,1,0:T(8,128)(2,1)S(1)}, bf16[2,64,144]{2,1,0:T(8,128)(2,1)}, u32[]{:S(2)}) %copy-start.2) | copy-done | bytes 36888
  2.7 0.0 copy-start.3
  2.7 1.1 %copy-done.3 = bf16[2,64,128]{2,1,0:T(8,128)(2,1)S(1)} copy-done((bf16[2,64,128]{2,1,0:T(8,128)(2,1)S(1)}, bf16[2,64,128]{2,1,0:T(8,128)(2,1)}, u32[]{:S(2)}) %copy-start.3) | copy-done | bytes 32792
  3.8 0.0 copy-start.4
  3.8 0.7 copy-done.4
  4.5 0.0 copy-start.5
  4.5 0.7 copy-done.5
  5.2 0.0 copy-start.6
  5.2 0.7 copy-done.6
  5.9 0.0 copy-start.7
  5.9 0.7 copy-done.7
  6.6 0.0 copy-start.8
  6.6 0.7 copy-done.8
  7.2 0.0 copy-start.9
  7.2 0.7 copy-done.9
  7.9 0.0 copy-start.10
  7.9 0.7 copy-done.10
  8.5 69.5 %gain.1 = (bf16[64,4608]{1,0:T(8,128)(2,1)S(1)}, bf16[576,64]{1,0:T(8,128)(2,1)S(1)}, f32[1,144]{1,0:T(1,128)S(1)}) custom-call(f32[576,4608]{1,0:T(8,128)} %bitcast.9, f32[1,144]{1,0:T(1,128)S(1)} %bitcast.11, bf16[2,64,144]{2,1,0:T(8,128)(2,1)S(1)} %copy-done.2, bf16[2,64,128]{2,1,0:T(8,128)(2,1)S(1)} %copy-done.3, s32[2,64,138]{2,1,0:T(8,128)S(1)} %copy-done.1, ...), custom_call_target="tpu_custom_call" | custom-call | tf_op jit(solution)/shard_map/gain/pallas_call | solution.py:502
  78.1 0.0 copy-done
  78.1 6.0 %update.1 = f32[576,4608]{1,0:T(8,128)} custom-call(f32[576,4608]{1,0:T(8,128)S(1)} %bitcast.10, bf16[64,4608]{1,0:T(8,128)(2,1)S(1)} %get-tuple-element.6.nt_ref, bf16[576,64]{1,0:T(8,128)(2,1)S(1)} %get-tuple-element.7.gt_ref), custom_call_target="tpu_custom_call" | custom-call | tf_op jit(solution)/shard_map/update/pallas_call | solution.py:588
  84.1 0.6 copy.15
Async XLA Ops:
  0.6 77.4 %copy-start = (f32[4608,576]{0,1:T(8,128)S(1)}, f32[4608,576]{0,1:T(8,128)}, u32[]{:S(2)}) copy-start(f32[4608,576]{0,1:T(8,128)} %param.11) | copy-start | bytes 31850500
  0.6 1.1 %copy-start.1 = (s32[2,64,138]{2,1,0:T(8,128)S(1)}, s32[2,64,138]{2,1,0:T(8,128)}, u32[]{:S(2)}) copy-start(s32[2,64,138]{2,1,0:T(8,128)} %nb_ref.1) | copy-start | bytes 211972
  1.7 1.0 %copy-start.2 = (bf16[2,64,144]{2,1,0:T(8,128)(2,1)S(1)}, bf16[2,64,144]{2,1,0:T(8,128)(2,1)}, u32[]{:S(2)}) copy-start(bf16[2,64,144]{2,1,0:T(8,128)(2,1)} %act_ref.1) | copy-start | bytes 110596
  2.7 1.1 %copy-start.3 = (bf16[2,64,128]{2,1,0:T(8,128)(2,1)S(1)}, bf16[2,64,128]{2,1,0:T(8,128)(2,1)}, u32[]{:S(2)}) copy-start(bf16[2,64,128]{2,1,0:T(8,128)(2,1)} %up_ref.1) | copy-start | bytes 98308
  3.8 0.7 copy-start.4
  4.5 0.7 copy-start.5
  5.2 0.7 copy-start.6
  5.9 0.7 copy-start.7
  6.6 0.7 copy-start.8
  7.2 0.7 copy-start.9
  7.9 0.7 copy-start.10

commit v3 on v2

--- a/solution.py
+++ b/solution.py
@@ -20,20 +20,26 @@
     rows,
     cols,
     cov_hbm,
-    weights_ref,
-    act_ref,
-    up_ref,
-    nb_ref,
-    types_ref,
-    tgain_ref,
-    sens_ref,
-    frame_ref,
-    noise_ref,
-    innov_ref,
+    weights_hbm,
+    act_hbm,
+    up_hbm,
+    nb_hbm,
+    types_hbm,
+    tgain_hbm,
+    sens_hbm,
+    frame_hbm,
+    noise_hbm,
+    innov_hbm,
     nt_ref,
     gt_ref,
     wnew_ref,
     cov_f,
+    weights_ref,
+    up_ref,
+    tgain_ref,
+    frame_ref,
+    noise_ref,
+    innov_ref,
     cov_hi,
     cov_lo,
     nb_all,
@@ -64,7 +70,9 @@
     n_own,
     s_mine,
     s_in,
+    load_sem,
     cov_sem,
+    row_in,
     sib_send,
     sib_recv,
     u_send,
@@ -102,14 +110,14 @@
     drains = []
     other = 1 - s
     sib = c + 1 - 2 * s
-    atoms = nb_ref.shape[1]
+    atoms = nb_hbm.shape[1]
     pair = 2 * atoms
-    nbr = nb_ref.shape[2]
-    adjw = up_ref.shape[2]
-    actw = act_ref.shape[2]
-    mg = sens_ref.shape[0]
+    nbr = nb_hbm.shape[2]
+    adjw = up_hbm.shape[2]
+    actw = act_hbm.shape[2]
+    mg = sens_hbm.shape[0]
     measures = mg * rows
-    width, chunk = cov_f.shape[1:]
+    width, chunk = cov_hi.shape[1:]
     bl = adjw // chips
 
     def remote(src, dst, ssem, rsem, tr, tc):
@@ -124,16 +132,51 @@
 
     cov_in = [
         pltpu.make_async_copy(
-            cov_hbm.at[:, pl.ds(j * chunk, chunk)], cov_f.at[j], cov_sem.at[j]
+            cov_hbm.at[:, pl.ds(j * chunk, chunk)],
+            cov_f.at[:, pl.ds(j * chunk, chunk)],
+            cov_sem.at[j],
         )
         for j in range(zs)
     ]
 
+    barrier = pltpu.get_barrier_semaphore()
+
+    def greet(k, _):
+        to = lax.rem(c + k, cols)
+        pl.semaphore_signal(barrier, inc=1, device_id=(r, to), device_id_type=MESH)
+        return 0
+
+    lax.fori_loop(1, cols, greet, 0)
+    for d in range(1, rows):
+        to = lax.rem(r + d, rows)
+        pl.semaphore_signal(barrier, inc=1, device_id=(to, c), device_id_type=MESH)
+    loads = [
+        pltpu.make_async_copy(src, dst, load_sem.at[i])
+        for i, (src, dst) in enumerate(
+            (
+                (up_hbm, up_ref),
+                (nb_hbm.at[s], nb_all.at[s]),
+                (act_hbm.at[s], act_pair.at[s]),
+                (sens_hbm, sens_pair.at[s]),
+                (types_hbm.at[s], kind_all.at[s]),
+                (tgain_hbm, tgain_ref),
+                (frame_hbm, frame_ref),
+                (noise_hbm, noise_ref),
+                (innov_hbm, innov_ref),
+                (weights_hbm, weights_ref),
+            )
+        )
+    ]
+    for load in loads:
+        load.start()
+    loads[0].wait()
+    pl.semaphore_wait(barrier, cols - 1 + rows - 1)
+
     sib_copies = [
-        remote(nb_ref.at[other], nb_all.at[s], sib_send.at[0], sib_recv.at[0], r, sib),
-        remote(act_ref.at[other], act_pair.at[s], sib_send.at[1], sib_recv.at[1], r, sib),
-        remote(sens_ref, sens_pair.at[s], sib_send.at[2], sib_recv.at[2], r, sib),
-        remote(types_ref.at[other], kind_all.at[s], sib_send.at[3], sib_recv.at[3], r, sib),
+        remote(nb_hbm.at[other], nb_all.at[s], sib_send.at[0], sib_recv.at[0], r, sib),
+        remote(act_hbm.at[other], act_pair.at[s], sib_send.at[1], sib_recv.at[1], r, sib),
+        remote(sens_hbm, sens_pair.at[s], sib_send.at[2], sib_recv.at[2], r, sib),
+        remote(types_hbm.at[other], kind_all.at[s], sib_send.at[3], sib_recv.at[3], r, sib),
     ]
     sib_copies[0].start()
     mine = pl.ds(pl.multiple_of(c * atoms, atoms), atoms)
@@ -154,10 +197,11 @@
     for copy in cov_in:
         copy.start()
 
-    nb_all[s] = nb_ref[s]
-    kind_all[s] = types_ref[s]
-    act_pair[s] = act_ref[s]
-    sens_pair[s] = sens_ref[...]
+    for d in range(1, rows):
+        to = lax.rem(r + d, rows)
+        pl.semaphore_signal(row_in, inc=1, device_id=(to, c), device_id_type=MESH)
+    for load in loads[1:]:
+        load.wait()
     sib_copies[1].wait_recv()
     sib_copies[2].wait_recv()
     act_t[...] = jnp.transpose(
@@ -211,23 +255,6 @@
     lax.fori_loop(0, pair // unroll, count, 0)
     for k in range(his):
         counts_b[:, k * 128 : (k + 1) * 128] = counts[k].astype(BF16)
-
-    strip = 64
-
-    def split(j):
-        def body(i, _):
-            at = pl.ds(pl.multiple_of(i * strip, strip), strip)
-            value = cov_f[j, at, :]
-            high = value.astype(BF16)
-            cov_hi[j, at, :] = high
-            cov_lo[j, at, :] = (value - high.astype(F32)).astype(BF16)
-            return 0
-
-        lax.fori_loop(0, width // strip, body, 0)
-
-    for j in range(zs):
-        cov_in[j].wait()
-        split(j)
 
     pltpu.make_async_copy(up_all, up_all, u_recv).wait()
     neighbor_sum = jnp.dot(
@@ -257,12 +284,30 @@
 
     drains.append(drain_adj)
 
+    strip = 64
+
+    def split(j):
+        def body(i, _):
+            at = pl.ds(pl.multiple_of(i * strip, strip), strip)
+            value = cov_f[at, j * chunk : (j + 1) * chunk]
+            high = value.astype(BF16)
+            cov_hi[j, at, :] = high
+            cov_lo[j, at, :] = (value - high.astype(F32)).astype(BF16)
+            return 0
+
+        lax.fori_loop(0, width // strip, body, 0)
+
+    for j in range(zs):
+        cov_in[j].wait()
+        split(j)
+
     pltpu.make_async_copy(sens_all, sens_all, sn_recv).wait()
-    which = lax.broadcasted_iota(jnp.int32, (mg, 1), 0)
-    frame_of = jnp.zeros((mg, 1), jnp.int32)
-    for m in range(mg):
-        frame_of = jnp.where(which == m, frame_ref[m], frame_of)
-    chosen = jnp.where(frame_of == s, 1.0, 0.0).astype(F32)
+    m0 = lax.broadcasted_iota(jnp.int32, (mg, mg), 0)
+    m1 = lax.broadcasted_iota(jnp.int32, (mg, mg), 1)
+    frame_of = jnp.sum(
+        jnp.where(m0 == m1, frame_ref[...].astype(F32), 0.0), axis=1, keepdims=True
+    )
+    chosen = jnp.where(frame_of == s.astype(F32), 1.0, 0.0)
     sens_all[...] = sens_all[...] * chosen
     pltpu.make_async_copy(act_all, act_all, a_recv).wait()
     pltpu.make_async_copy(adj_all, adj_all, ad_recv).wait()
@@ -351,6 +396,7 @@
 
         lax.fori_loop(0, half, step, 0)
 
+    pl.semaphore_wait(row_in, rows - 1)
     cast(jac_piece, jac_all, 0)
     relay(jac_all, 0)
 
@@ -412,21 +458,31 @@
             remote(n_slices.at[t], n_own.at[r], o_send.at[t], o_recv.at[r], x, to).start()
 
     relay(nt_ref, 1)
-    relayed(nt_ref, 1)
-
-    s_mine[...] = lax.dot_general(
-        jac_all[...], nt_ref[...], NT, preferred_element_type=F32
-    )
-    for d in range(1, rows):
-        to = lax.rem(r + d, rows)
-        copy = remote(s_mine, s_in.at[d - 1], s_send.at[d - 1], s_recv.at[d - 1], to, c)
+
+    partial = jnp.zeros((measures, measures), F32)
+    for i in range(zs // 2):
+        lanes = pl.ds(pl.multiple_of(chunk * (2 * i + parity), chunk), chunk)
+        partial = partial + lax.dot_general(
+            jac_all[:, lanes], nt_ref[:, lanes], NT, preferred_element_type=F32
+        )
+    top = measures // 2
+    s_mine[...] = jnp.concatenate([partial[:top], partial[top:]], axis=1)
+    group = 2 * rows
+    for d in range(1, group):
+        to = lax.rem(2 * r + s + d, group)
+        copy = remote(
+            s_mine, s_in.at[d - 1], s_send.at[d - 1], s_recv.at[d - 1], to // 2, 2 * h + to % 2
+        )
         copy.start()
         drains.append(copy.wait_send)
-    for d in range(1, rows):
+    for d in range(1, group):
         pltpu.make_async_copy(s_in.at[d - 1], s_in.at[d - 1], s_recv.at[d - 1]).wait()
-    innovation_cov = s_mine[...]
-    for d in range(1, rows):
-        innovation_cov = innovation_cov + s_in[d - 1]
+    packed = s_mine[...]
+    for d in range(1, group):
+        packed = packed + s_in[d - 1]
+    innovation_cov = jnp.concatenate(
+        [packed[:, :measures], packed[:, measures:]], axis=0
+    )
     i0 = lax.broadcasted_iota(jnp.int32, (measures, measures), 0)
     i1 = lax.broadcasted_iota(jnp.int32, (measures, measures), 1)
     eye = jnp.where(i0 == i1, 1.0, 0.0).astype(F32)
@@ -457,12 +513,15 @@
         def _():
             pltpu.make_async_copy(n_slices.at[t], n_slices.at[t], o_send.at[t]).wait()
 
+    relayed(nt_ref, 1)
     for drain in drains:
         drain()
 
 
 def update_kernel(cov_ref, nt_ref, gt_ref, out_ref):
-    out_ref[...] = cov_ref[...] - jnp.dot(
+    tile = out_ref.shape[0]
+    at = pl.ds(pl.multiple_of(pl.program_id(0) * tile, tile), tile)
+    out_ref[...] = cov_ref[at, :] - jnp.dot(
         gt_ref[...], nt_ref[...], preferred_element_type=F32
     )
 
@@ -498,21 +557,23 @@
     his = all_atoms // 128
     dma = pltpu.SemaphoreType.DMA
     vmem = pl.BlockSpec(memory_space=pltpu.VMEM)
-    covariance = cov.T
-    n_rows, gain, weights_new = pl.pallas_call(
+    n_rows, gain, weights_new, block = pl.pallas_call(
         functools.partial(gain_kernel, rows, cols),
         out_shape=(
             jax.ShapeDtypeStruct((measures, height), BF16),
             jax.ShapeDtypeStruct((width, measures), BF16),
             jax.ShapeDtypeStruct((1, owned), F32),
+            jax.ShapeDtypeStruct((width, height), F32),
         ),
-        in_specs=[pl.BlockSpec(memory_space=pl.ANY)]
-        + [vmem] * 7
-        + [pl.BlockSpec(memory_space=pltpu.SMEM)]
-        + [vmem] * 2,
-        out_specs=(vmem,) * 3,
+        in_specs=[pl.BlockSpec(memory_space=pltpu.HBM)] * 11,
+        out_specs=(vmem,) * 4,
         scratch_shapes=[
-            pltpu.VMEM((zs, width, chunk), F32),
+            pltpu.VMEM((1, owned), F32),
+            pltpu.VMEM((frames, atoms, adjw), BF16),
+            pltpu.VMEM(type_gain.shape, F32),
+            pltpu.VMEM((1, mg), jnp.int32),
+            pltpu.VMEM((1, measures), F32),
+            pltpu.VMEM((1, measures), F32),
             pltpu.VMEM((zs, width, chunk), BF16),
             pltpu.VMEM((zs, width, chunk), BF16),
             pltpu.VMEM((2, atoms, nbr), jnp.int32),
@@ -541,9 +602,11 @@
             pltpu.VMEM((rows, mg, width), BF16),
             pltpu.VMEM((rows, mg, owned), F32),
             pltpu.VMEM((rows, mg, owned), F32),
-            pltpu.VMEM((measures, measures), F32),
-            pltpu.VMEM((rows - 1, measures, measures), F32),
+            pltpu.VMEM((measures // 2, 2 * measures), F32),
+            pltpu.VMEM((2 * rows - 1, measures // 2, 2 * measures), F32),
+            dma((10,)),
             dma((zs,)),
+            pltpu.SemaphoreType.REGULAR,
             dma((6,)),
             dma((6,)),
             dma,
@@ -564,15 +627,15 @@
             dma((rows - 1,)),
             dma((rows,)),
             dma((rows,)),
-            dma((rows - 1,)),
-            dma((rows - 1,)),
+            dma((2 * rows - 1,)),
+            dma((2 * rows - 1,)),
         ],
         compiler_params=pltpu.CompilerParams(
-            has_side_effects=True, vmem_limit_bytes=52 * 2**20
+            collective_id=0, has_side_effects=True, vmem_limit_bytes=40 * 2**20
         ),
         name="gain",
     )(
-        covariance,
+        cov.T,
         weights.reshape(1, owned),
         act,
         upstream,
@@ -580,7 +643,7 @@
         types.reshape(frames, 1, atoms),
         type_gain,
         sens,
-        frame_for_measure,
+        frame_for_measure.reshape(1, mg),
         noise_variance.reshape(1, measures),
         innovation.reshape(1, measures),
     )
@@ -589,7 +652,7 @@
         update_kernel,
         grid=(per,),
         in_specs=[
-            pl.BlockSpec((tile, height), lambda j: (j, 0)),
+            pl.BlockSpec(memory_space=pltpu.VMEM),
             pl.BlockSpec((measures, height), lambda j: (0, 0)),
             pl.BlockSpec((tile, measures), lambda j: (j, 0)),
         ],
@@ -597,7 +660,7 @@
         out_shape=jax.ShapeDtypeStruct((width, height), F32),
         compiler_params=pltpu.CompilerParams(vmem_limit_bytes=32 * 2**20),
         name="update",
-    )(covariance, n_rows, gain)
+    )(block, n_rows, gain)
     return weights_new.reshape(owned), cov_new.T
 
 

time: 85.1 us -> 80.3 us (0.944)
  Pallas kernels: 75.6 us -> 71.5 us
    pallas_call x1, Pallas kernels: 69.5 us -> 65.5 us  [on_device(): pl.pallas_call(functools.partial(gain_kernel, rows, cols), out_shape=(jax...]
    unnamed x23 -> x21, local copies, waits for them, and re-layouts: 8.44 us -> 7.75 us
where the time goes in v3:
time: 80.3 us; the launch traced here: 79.9 us
  Pallas kernels  71.5 us (89%)
  local copies, waits for them, and re-layouts  7.75 us (10%)
    pallas_call x1, Pallas kernels, on_device(): pl.pallas_call(functools.partial(gain_kernel, rows, cols), out_shape=(jax...  65.5 us
    unnamed x21, local copies, waits for them, and re-layouts  7.75 us
    pallas_call x1, Pallas kernels, on_device(): pl.pallas_call(update_kernel, grid=(per,), in_specs=[pl.BlockSpec(memory_...  6.02 us

profile of v3, /device:TPU:1, one launch (start us, length us, event | category | flops | bytes accessed | tf_op | source)
XLA Modules:
  0.0 79.9 jit_solution(7945101106469628642)
XLA Ops:
  0.6 0.0 copy-start
  0.6 0.9 %copy-done = s32[2,64,138]{2,1,0:T(8,128)S(1)} copy-done((s32[2,64,138]{2,1,0:T(8,128)S(1)}, s32[2,64,138]{2,1,0:T(8,128)}, u32[]{:S(2)}) %copy-start) | copy-done | bytes 70680
  1.5 0.0 copy-start.1
  1.5 0.8 %copy-done.1 = bf16[2,64,144]{2,1,0:T(8,128)(2,1)S(1)} copy-done((bf16[2,64,144]{2,1,0:T(8,128)(2,1)S(1)}, bf16[2,64,144]{2,1,0:T(8,128)(2,1)}, u32[]{:S(2)}) %copy-start.1) | copy-done | bytes 36888
  2.4 0.0 copy-start.2
  2.4 0.8 copy-done.2
  3.1 0.0 copy-start.3
  3.1 0.7 copy-done.3
  3.8 0.0 copy-start.4
  3.8 0.7 copy-done.4
  4.5 0.0 copy-start.5
  4.5 0.7 copy-done.5
  5.2 0.0 copy-start.6
  5.2 0.7 copy-done.6
  5.9 0.0 copy-start.7
  5.9 0.7 copy-done.7
  6.5 0.0 copy-start.8
  6.5 0.7 copy-done.8
  7.2 0.0 copy-start.9
  7.2 0.7 copy-done.9
  7.8 65.5 %gain.1 = (bf16[64,4608]{1,0:T(8,128)(2,1)S(1)}, bf16[576,64]{1,0:T(8,128)(2,1)S(1)}, f32[1,144]{1,0:T(1,128)S(1)}, f32[576,4608]{1,0:T(8,128)S(1)}) custom-call(f32[576,4608]{1,0:T(8,128)} %bitcast.17, f32[1,144]{1,0:T(1,128)S(1)} %bitcast.10, bf16[2,64,144]{2,1,0:T(8,128)(2,1)S(1)} %copy-done.1, bf16[2,64,128]{2,1,0:T(8,128)(2,1)S(1)} %copy-done.2, ...), custom_call_target="tpu_custom_call" | custom-call | tf_op jit(solution)/shard_map/gain/pallas_call | solution.py:560
  73.3 6.0 %update.1 = f32[576,4608]{1,0:T(8,128)} custom-call(f32[576,4608]{1,0:T(8,128)S(1)} %get-tuple-element.7.cov_ref, bf16[64,4608]{1,0:T(8,128)(2,1)S(1)} %get-tuple-element.8.nt_ref, bf16[576,64]{1,0:T(8,128)(2,1)S(1)} %get-tuple-element.9.gt_ref), custom_call_target="tpu_custom_call" | custom-call | tf_op jit(solution)/shard_map/update/pallas_call | solution.py:651
  79.4 0.6 copy.15
Async XLA Ops:
  0.6 0.9 %copy-start = (s32[2,64,138]{2,1,0:T(8,128)S(1)}, s32[2,64,138]{2,1,0:T(8,128)}, u32[]{:S(2)}) copy-start(s32[2,64,138]{2,1,0:T(8,128)} %nb_hbm.1) | copy-start | bytes 211972
  1.5 0.8 %copy-start.1 = (bf16[2,64,144]{2,1,0:T(8,128)(2,1)S(1)}, bf16[2,64,144]{2,1,0:T(8,128)(2,1)}, u32[]{:S(2)}) copy-start(bf16[2,64,144]{2,1,0:T(8,128)(2,1)} %act_hbm.1) | copy-start | bytes 110596
  2.4 0.8 copy-start.2
  3.1 0.7 copy-start.3
  3.8 0.7 copy-start.4
  4.5 0.7 copy-start.5
  5.2 0.7 copy-start.6
  5.9 0.7 copy-start.7
  6.5 0.7 copy-start.8
  7.2 0.7 copy-start.9

commit v4 on v3

--- a/solution.py
+++ b/solution.py
@@ -49,9 +49,7 @@
     counts,
     counts_b,
     up_all,
-    act_t,
     act_all,
-    sens_row,
     sens_all,
     adj_t,
     adj_all,
@@ -68,8 +66,11 @@
     n_col,
     n_slices,
     n_own,
-    s_mine,
-    s_in,
+    jac_own,
+    jac_col,
+    t_mine,
+    t_in,
+    t_rows,
     load_sem,
     cov_sem,
     row_in,
@@ -77,6 +78,8 @@
     sib_recv,
     u_send,
     u_recv,
+    a_first,
+    sn_first,
     a_send,
     a_recv,
     sn_send,
@@ -93,8 +96,12 @@
     c_recv,
     o_send,
     o_recv,
-    s_send,
-    s_recv,
+    j_send,
+    j_recv,
+    t_send,
+    t_recv,
+    q_send,
+    q_recv,
 ):
     r = lax.axis_index("row")
     c = lax.axis_index("col")
@@ -139,17 +146,6 @@
         for j in range(zs)
     ]
 
-    barrier = pltpu.get_barrier_semaphore()
-
-    def greet(k, _):
-        to = lax.rem(c + k, cols)
-        pl.semaphore_signal(barrier, inc=1, device_id=(r, to), device_id_type=MESH)
-        return 0
-
-    lax.fori_loop(1, cols, greet, 0)
-    for d in range(1, rows):
-        to = lax.rem(r + d, rows)
-        pl.semaphore_signal(barrier, inc=1, device_id=(to, c), device_id_type=MESH)
     loads = [
         pltpu.make_async_copy(src, dst, load_sem.at[i])
         for i, (src, dst) in enumerate(
@@ -169,6 +165,17 @@
     ]
     for load in loads:
         load.start()
+    barrier = pltpu.get_barrier_semaphore()
+
+    def greet(k, _):
+        to = lax.rem(c + k, cols)
+        pl.semaphore_signal(barrier, inc=1, device_id=(r, to), device_id_type=MESH)
+        return 0
+
+    lax.fori_loop(1, cols, greet, 0)
+    for d in range(1, rows):
+        to = lax.rem(r + d, rows)
+        pl.semaphore_signal(barrier, inc=1, device_id=(to, c), device_id_type=MESH)
     loads[0].wait()
     pl.semaphore_wait(barrier, cols - 1 + rows - 1)
 
@@ -204,32 +211,49 @@
         load.wait()
     sib_copies[1].wait_recv()
     sib_copies[2].wait_recv()
-    act_t[...] = jnp.transpose(
+    def lanes_of(chip):
+        return pl.ds(pl.multiple_of(chip * pair, pair), pair)
+
+    lanes_mine = lanes_of(h)
+    act_all[:, lanes_mine] = jnp.transpose(
         act_pair[...].reshape(pair, actw).astype(F32)
     ).astype(BF16)
-    sens_row[...] = jnp.concatenate([sens_pair[0], sens_pair[1]], axis=1)
-    lanes_mine = pl.ds(pl.multiple_of(h * pair, pair), pair)
-    own_act = pltpu.make_async_copy(act_t, act_all.at[:, lanes_mine], a_recv)
-    own_sens = pltpu.make_async_copy(sens_row, sens_all.at[:, lanes_mine], sn_recv)
-    own_act.start()
-    own_sens.start()
-
-    def send_act(k, _):
-        to = 2 * lax.rem(h + k, chips) + s
-        remote(act_t, act_all.at[:, lanes_mine], a_send, a_recv, r, to).start()
-        remote(sens_row, sens_all.at[:, lanes_mine], sn_send, sn_recv, r, to).start()
-        return 0
-
-    lax.fori_loop(1, chips, send_act, 0)
+    sens_all[:, lanes_mine] = jnp.concatenate([sens_pair[0], sens_pair[1]], axis=1)
+
+    def along(axis_is_z, d):
+        in_z = x * zs + lax.rem(z + d + zs, zs)
+        in_x = lax.rem(x + d + zs, zs) * zs + z
+        return jnp.where(axis_is_z, in_z, in_x)
+
+    first_z = s == 0
+    second_z = s == 1
+    tree = ((act_all, a_first, a_send, a_recv), (sens_all, sn_first, sn_send, sn_recv))
+    for d in range(1, zs):
+        to = 2 * along(first_z, d) + s
+        for buf, first, send, recv in tree:
+            part = buf.at[:, lanes_mine]
+            remote(part, part, send, first.at[d - 1], r, to).start()
+
+    def spread_line(e):
+        lanes = lanes_of(along(first_z, -e))
+        for buf, first, send, recv in tree:
+            part = buf.at[:, lanes]
+            if e > 0:
+                pltpu.make_async_copy(part, part, first.at[e - 1]).wait()
+            for d in range(1, zs):
+                to = 2 * along(second_z, d) + s
+                remote(part, part, send, recv, r, to).start()
+
+    spread_line(0)
 
     def drain_first():
         for copy in sib_copies:
             copy.wait_send()
         sent_up = up_all.at[pl.ds(0, (2 * chips - 1) * atoms)]
         pltpu.make_async_copy(sent_up, sent_up, u_send).wait()
-        for buf, sem in ((act_all, a_send), (sens_all, sn_send)):
+        for buf, _, send, _ in tree:
             part = buf.at[:, pl.ds(0, (chips - 1) * pair)]
-            pltpu.make_async_copy(part, part, sem).wait()
+            pltpu.make_async_copy(part, part, send).wait()
 
     drains.append(drain_first)
 
@@ -255,6 +279,9 @@
     lax.fori_loop(0, pair // unroll, count, 0)
     for k in range(his):
         counts_b[:, k * 128 : (k + 1) * 128] = counts[k].astype(BF16)
+
+    for e in range(1, zs):
+        spread_line(e)
 
     pltpu.make_async_copy(up_all, up_all, u_recv).wait()
     neighbor_sum = jnp.dot(
@@ -301,18 +328,19 @@
         cov_in[j].wait()
         split(j)
 
-    pltpu.make_async_copy(sens_all, sens_all, sn_recv).wait()
+    for buf, _, _, recv in tree[::-1]:
+        part = buf.at[:, pl.ds(0, (chips - zs) * pair)]
+        pltpu.make_async_copy(part, part, recv).wait()
     m0 = lax.broadcasted_iota(jnp.int32, (mg, mg), 0)
     m1 = lax.broadcasted_iota(jnp.int32, (mg, mg), 1)
     frame_of = jnp.sum(
         jnp.where(m0 == m1, frame_ref[...].astype(F32), 0.0), axis=1, keepdims=True
     )
     chosen = jnp.where(frame_of == s.astype(F32), 1.0, 0.0)
-    sens_all[...] = sens_all[...] * chosen
-    pltpu.make_async_copy(act_all, act_all, a_recv).wait()
+    sens_own = sens_all[...] * chosen
     pltpu.make_async_copy(adj_all, adj_all, ad_recv).wait()
     for b in range(bl):
-        w_rows[mg * b : mg * (b + 1), :] = (sens_all[...] * adj_all[b : b + 1, :]).astype(BF16)
+        w_rows[mg * b : mg * (b + 1), :] = (sens_own * adj_all[b : b + 1, :]).astype(BF16)
     jac_half[...] = lax.dot_general(
         w_rows[...], act_all[...], NT, preferred_element_type=F32
     )
@@ -324,6 +352,12 @@
         [whole[mg * b : mg * (b + 1), :] for b in range(bl)], axis=1
     ).astype(BF16)
     drains.append(swap.wait_send)
+    rows_half = bl * mg // 2
+    own_half = jnp.where(s == 0, whole[:rows_half], whole[rows_half:])
+    jac_own[...] = jnp.concatenate(
+        [own_half[mg * b : mg * (b + 1), :] for b in range(bl // 2)], axis=1
+    ).astype(BF16)
+    jac_col[r] = jac_own[...]
 
     half = chips // 2
 
@@ -398,6 +432,11 @@
 
     pl.semaphore_wait(row_in, rows - 1)
     cast(jac_piece, jac_all, 0)
+    for d in range(1, rows):
+        to = lax.rem(r + d, rows)
+        copy = remote(jac_own, jac_col.at[r], j_send.at[d - 1], j_recv.at[d - 1], to, c)
+        copy.start()
+        drains.append(copy.wait_send)
     relay(jac_all, 0)
 
     def times(which):
@@ -437,6 +476,28 @@
         copy = remote(n_piece, n_col.at[r], c_send.at[d - 1], c_recv.at[d - 1], to, c)
         copy.start()
         drains.append(copy.wait_send)
+    for d in range(1, rows):
+        pltpu.make_async_copy(jac_own, jac_own, j_recv.at[d - 1]).wait()
+    n_low = (mine_n - n_piece[...].astype(F32)).astype(BF16)
+    jac_here = jac_col[...].reshape(measures, width)
+    part = lax.dot_general(
+        n_piece[...], jac_here, NT, preferred_element_type=F32
+    ) + lax.dot_general(n_low, jac_here, NT, preferred_element_type=F32)
+    t_mine[...] = jnp.concatenate([part[: mg // 2], part[mg // 2 :]], axis=1)
+    t_in[c] = t_mine[...]
+
+    def send_part(k, _):
+        to = lax.rem(c + k, cols)
+        remote(t_mine, t_in.at[c], t_send, t_recv, r, to).start()
+        return 0
+
+    lax.fori_loop(1, cols, send_part, 0)
+
+    def drain_part():
+        sent = t_in.at[pl.ds(0, cols - 1)]
+        pltpu.make_async_copy(sent, sent, t_send).wait()
+
+    drains.append(drain_part)
     swap_n.wait_recv()
     n_wide[...] = jnp.concatenate(
         [n_pair[0].astype(F32), n_pair[1].astype(F32)], axis=1
@@ -457,32 +518,22 @@
         def _():
             remote(n_slices.at[t], n_own.at[r], o_send.at[t], o_recv.at[r], x, to).start()
 
-    relay(nt_ref, 1)
-
-    partial = jnp.zeros((measures, measures), F32)
-    for i in range(zs // 2):
-        lanes = pl.ds(pl.multiple_of(chunk * (2 * i + parity), chunk), chunk)
-        partial = partial + lax.dot_general(
-            jac_all[:, lanes], nt_ref[:, lanes], NT, preferred_element_type=F32
-        )
-    top = measures // 2
-    s_mine[...] = jnp.concatenate([partial[:top], partial[top:]], axis=1)
-    group = 2 * rows
-    for d in range(1, group):
-        to = lax.rem(2 * r + s + d, group)
-        copy = remote(
-            s_mine, s_in.at[d - 1], s_send.at[d - 1], s_recv.at[d - 1], to // 2, 2 * h + to % 2
-        )
+    arrived = t_in.at[pl.ds(0, cols - 1)]
+    pltpu.make_async_copy(arrived, arrived, t_recv).wait()
+    t_rows[r] = jnp.sum(t_in[...], axis=0)
+    for d in range(1, rows):
+        to = lax.rem(r + d, rows)
+        copy = remote(t_rows.at[r], t_rows.at[r], q_send.at[d - 1], q_recv.at[d - 1], to, c)
         copy.start()
         drains.append(copy.wait_send)
-    for d in range(1, group):
-        pltpu.make_async_copy(s_in.at[d - 1], s_in.at[d - 1], s_recv.at[d - 1]).wait()
-    packed = s_mine[...]
-    for d in range(1, group):
-        packed = packed + s_in[d - 1]
-    innovation_cov = jnp.concatenate(
-        [packed[:, :measures], packed[:, measures:]], axis=0
-    )
+    relay(nt_ref, 1)
+    for d in range(1, rows):
+        pltpu.make_async_copy(t_rows.at[0], t_rows.at[0], q_recv.at[d - 1]).wait()
+    pieces = []
+    for q in range(rows):
+        packed = t_rows[q]
+        pieces += [packed[:, :measures], packed[:, measures:]]
+    innovation_cov = jnp.concatenate(pieces, axis=0)
     i0 = lax.broadcasted_iota(jnp.int32, (measures, measures), 0)
     i1 = lax.broadcasted_iota(jnp.int32, (measures, measures), 1)
     eye = jnp.where(i0 == i1, 1.0, 0.0).astype(F32)
@@ -519,9 +570,7 @@
 
 
 def update_kernel(cov_ref, nt_ref, gt_ref, out_ref):
-    tile = out_ref.shape[0]
-    at = pl.ds(pl.multiple_of(pl.program_id(0) * tile, tile), tile)
-    out_ref[...] = cov_ref[at, :] - jnp.dot(
+    out_ref[...] = cov_ref[...] - jnp.dot(
         gt_ref[...], nt_ref[...], preferred_element_type=F32
     )
 
@@ -583,9 +632,7 @@
             pltpu.VMEM((his, pair, 128), F32),
             pltpu.VMEM((pair, all_atoms), BF16),
             pltpu.VMEM((all_atoms, adjw), BF16),
-            pltpu.VMEM((actw, pair), BF16),
             pltpu.VMEM((actw, all_atoms), BF16),
-            pltpu.VMEM((mg, pair), F32),
             pltpu.VMEM((mg, all_atoms), F32),
             pltpu.VMEM((chips, bl, pair), F32),
             pltpu.VMEM((bl, all_atoms), F32),
@@ -602,8 +649,11 @@
             pltpu.VMEM((rows, mg, width), BF16),
             pltpu.VMEM((rows, mg, owned), F32),
             pltpu.VMEM((rows, mg, owned), F32),
-            pltpu.VMEM((measures // 2, 2 * measures), F32),
-            pltpu.VMEM((2 * rows - 1, measures // 2, 2 * measures), F32),
+            pltpu.VMEM((mg, width), BF16),
+            pltpu.VMEM((rows, mg, width), BF16),
+            pltpu.VMEM((mg // 2, 2 * measures), F32),
+            pltpu.VMEM((cols, mg // 2, 2 * measures), F32),
+            pltpu.VMEM((rows, mg // 2, 2 * measures), F32),
             dma((10,)),
             dma((zs,)),
             pltpu.SemaphoreType.REGULAR,
@@ -611,6 +661,8 @@
             dma((6,)),
             dma,
             dma,
+            dma((zs - 1,)),
+            dma((zs - 1,)),
             dma,
             dma,
             dma,
@@ -627,36 +679,45 @@
             dma((rows - 1,)),
             dma((rows,)),
             dma((rows,)),
-            dma((2 * rows - 1,)),
-            dma((2 * rows - 1,)),
+            dma((rows - 1,)),
+            dma((rows - 1,)),
+            dma,
+            dma,
+            dma((rows - 1,)),
+            dma((rows - 1,)),
         ],
         compiler_params=pltpu.CompilerParams(
             collective_id=0, has_side_effects=True, vmem_limit_bytes=40 * 2**20
         ),
         name="gain",
     )(
-        cov.T,
-        weights.reshape(1, owned),
-        act,
-        upstream,
-        neighbors,
-        types.reshape(frames, 1, atoms),
-        type_gain,
-        sens,
-        frame_for_measure.reshape(1, mg),
-        noise_variance.reshape(1, measures),
-        innovation.reshape(1, measures),
+        *(
+            pltpu.with_memory_space_constraint(array, pltpu.HBM)
+            for array in (
+                cov.T,
+                weights.reshape(1, owned),
+                act,
+                upstream,
+                neighbors,
+                types.reshape(frames, 1, atoms),
+                type_gain,
+                sens,
+                frame_for_measure.reshape(1, mg),
+                noise_variance.reshape(1, measures),
+                innovation.reshape(1, measures),
+            )
+        )
     )
-    tile = width // per
+    strip = height // 9
     cov_new = pl.pallas_call(
         update_kernel,
-        grid=(per,),
+        grid=(9,),
         in_specs=[
-            pl.BlockSpec(memory_space=pltpu.VMEM),
-            pl.BlockSpec((measures, height), lambda j: (0, 0)),
-            pl.BlockSpec((tile, measures), lambda j: (j, 0)),
+            pl.BlockSpec((width, strip), lambda j: (0, j)),
+            pl.BlockSpec((measures, strip), lambda j: (0, j)),
+            pl.BlockSpec((width, measures), lambda j: (0, 0)),
         ],
-        out_specs=pl.BlockSpec((tile, height), lambda j: (j, 0)),
+        out_specs=pl.BlockSpec((width, strip), lambda j: (0, j)),
         out_shape=jax.ShapeDtypeStruct((width, height), F32),
         compiler_params=pltpu.CompilerParams(vmem_limit_bytes=32 * 2**20),
         name="update",

time: 80.3 us -> 64.8 us (0.81)
  the two profiles are of different devices: /device:TPU:1 before, /device:TPU:5 now
where the time goes in v4:
time: 64.8 us; the launch traced here: 64.7 us
  Pallas kernels  63.5 us (98%)
    pallas_call x1, Pallas kernels, on_device(): pl.pallas_call(functools.partial(gain_kernel, rows, cols), out_shape=(jax...  56.5 us
    pallas_call x1, Pallas kernels, on_device(): pl.pallas_call(update_kernel, grid=(9,), in_specs=[pl.BlockSpec((width, s...  6.95 us

profile of v4, /device:TPU:5, one launch (start us, length us, event | category | flops | bytes accessed | tf_op | source)
XLA Modules:
  0.0 64.7 jit_solution(13544907967921697865)
XLA Ops:
  0.6 56.5 %gain.1 = (bf16[64,4608]{1,0:T(8,128)(2,1)S(1)}, bf16[576,64]{1,0:T(8,128)(2,1)S(1)}, f32[1,144]{1,0:T(1,128)S(1)}, f32[576,4608]{1,0:T(8,128)S(1)}) custom-call(f32[576,4608]{1,0:T(8,128)} %bitcast.12, f32[1,144]{1,0:T(1,128)} %bitcast.13, bf16[2,64,144]{2,1,0:T(8,128)(2,1)} %act_hbm.1, bf16[2,64,128]{2,1,0:T(8,128)(2,1)} %up_hbm.1, s32[2,64,138]{2,1,0:T(8,128)} %nb_hbm.1, ...), custom_call_target="tpu_custom_call" | custom-call | tf_op jit(solution)/shard_map/gain/pallas_call | solution.py:609
  57.2 6.9 %update.1 = f32[576,4608]{1,0:T(8,128)} custom-call(f32[576,4608]{1,0:T(8,128)S(1)} %get-tuple-element.7.cov_ref, bf16[64,4608]{1,0:T(8,128)(2,1)S(1)} %get-tuple-element.8.nt_ref, bf16[576,64]{1,0:T(8,128)(2,1)S(1)} %get-tuple-element.9.gt_ref), custom_call_target="tpu_custom_call" | custom-call | tf_op jit(solution)/shard_map/update/pallas_call | solution.py:712
  64.1 0.6 copy.15

commit v5 on v4

--- a/solution.py
+++ b/solution.py
@@ -35,7 +35,6 @@
     wnew_ref,
     cov_f,
     weights_ref,
-    up_ref,
     tgain_ref,
     frame_ref,
     noise_ref,
@@ -76,6 +75,7 @@
     row_in,
     sib_send,
     sib_recv,
+    u_first,
     u_send,
     u_recv,
     a_first,
@@ -146,11 +146,12 @@
         for j in range(zs)
     ]
 
+    mine = pl.ds(pl.multiple_of(c * atoms, atoms), atoms)
     loads = [
         pltpu.make_async_copy(src, dst, load_sem.at[i])
         for i, (src, dst) in enumerate(
             (
-                (up_hbm, up_ref),
+                (up_hbm.at[s], up_all.at[mine]),
                 (nb_hbm.at[s], nb_all.at[s]),
                 (act_hbm.at[s], act_pair.at[s]),
                 (sens_hbm, sens_pair.at[s]),
@@ -163,21 +164,23 @@
             )
         )
     ]
-    for load in loads:
+    barrier = pltpu.get_barrier_semaphore()
+
+    def along(in_z, d):
+        z_line = x * zs + lax.rem(z + d + zs, zs)
+        x_line = lax.rem(x + d + zs, zs) * zs + z
+        return jnp.where(in_z, z_line, x_line)
+
+    line_mates = [(r, sib)]
+    for d in range(1, zs):
+        line_mates += [(r, 2 * along(True, d) + s), (r, 2 * along(False, d) + s)]
+    for d in range(1, rows):
+        line_mates.append((lax.rem(r + d, rows), c))
+    for mate in line_mates:
+        pl.semaphore_signal(barrier, inc=1, device_id=mate, device_id_type=MESH)
+    for load in loads + cov_in:
         load.start()
-    barrier = pltpu.get_barrier_semaphore()
-
-    def greet(k, _):
-        to = lax.rem(c + k, cols)
-        pl.semaphore_signal(barrier, inc=1, device_id=(r, to), device_id_type=MESH)
-        return 0
-
-    lax.fori_loop(1, cols, greet, 0)
-    for d in range(1, rows):
-        to = lax.rem(r + d, rows)
-        pl.semaphore_signal(barrier, inc=1, device_id=(to, c), device_id_type=MESH)
-    loads[0].wait()
-    pl.semaphore_wait(barrier, cols - 1 + rows - 1)
+    pl.semaphore_wait(barrier, len(line_mates))
 
     sib_copies = [
         remote(nb_hbm.at[other], nb_all.at[s], sib_send.at[0], sib_recv.at[0], r, sib),
@@ -185,74 +188,64 @@
         remote(sens_hbm, sens_pair.at[s], sib_send.at[2], sib_recv.at[2], r, sib),
         remote(types_hbm.at[other], kind_all.at[s], sib_send.at[3], sib_recv.at[3], r, sib),
     ]
-    sib_copies[0].start()
-    mine = pl.ds(pl.multiple_of(c * atoms, atoms), atoms)
-    own_up = pltpu.make_async_copy(up_ref.at[s], up_all.at[mine], u_recv)
-    own_up.start()
-    remote(up_ref.at[other], up_all.at[mine], u_send, u_recv, r, sib).start()
-
-    def send_up(k, _):
-        to = lax.rem(h + k, chips)
-        for f in range(2):
-            remote(up_ref.at[f], up_all.at[mine], u_send, u_recv, r, 2 * to + f).start()
-        return 0
-
-    lax.fori_loop(1, chips, send_up, 0)
-    sib_copies[1].start()
-    sib_copies[2].start()
-    sib_copies[3].start()
-    for copy in cov_in:
+    sib_up = remote(up_hbm.at[other], up_all.at[mine], sib_send.at[6], sib_recv.at[6], r, sib)
+    sib_up.start()
+    for copy in sib_copies:
         copy.start()
 
-    for d in range(1, rows):
-        to = lax.rem(r + d, rows)
-        pl.semaphore_signal(row_in, inc=1, device_id=(to, c), device_id_type=MESH)
+    def lanes_of(chip):
+        return pl.ds(pl.multiple_of(chip * pair, pair), pair)
+
+    lanes_mine = lanes_of(h)
+    begin_z = s == 0
+    then_z = s == 1
+    up_tree = (lambda chip: up_all.at[lanes_of(chip)], u_first, u_send, u_recv)
+    act_tree = (lambda chip: act_all.at[:, lanes_of(chip)], a_first, a_send, a_recv)
+    sens_tree = (lambda chip: sens_all.at[:, lanes_of(chip)], sn_first, sn_send, sn_recv)
+
+    def begin(tree):
+        block, first, send, recv = tree
+        part = block(h)
+        for d in range(1, zs):
+            remote(part, part, send, first.at[d - 1], r, 2 * along(begin_z, d) + s).start()
+
+    def spread_line(tree, e):
+        block, first, send, recv = tree
+        part = block(along(begin_z, -e))
+        if e > 0:
+            pltpu.make_async_copy(part, part, first.at[e - 1]).wait()
+        for d in range(1, zs):
+            remote(part, part, send, recv, r, 2 * along(then_z, d) + s).start()
+
+    loads[0].wait()
+    sib_up.wait_recv()
+    begin(up_tree)
+    spread_line(up_tree, 0)
     for load in loads[1:]:
         load.wait()
     sib_copies[1].wait_recv()
     sib_copies[2].wait_recv()
-    def lanes_of(chip):
-        return pl.ds(pl.multiple_of(chip * pair, pair), pair)
-
-    lanes_mine = lanes_of(h)
     act_all[:, lanes_mine] = jnp.transpose(
         act_pair[...].reshape(pair, actw).astype(F32)
     ).astype(BF16)
     sens_all[:, lanes_mine] = jnp.concatenate([sens_pair[0], sens_pair[1]], axis=1)
-
-    def along(axis_is_z, d):
-        in_z = x * zs + lax.rem(z + d + zs, zs)
-        in_x = lax.rem(x + d + zs, zs) * zs + z
-        return jnp.where(axis_is_z, in_z, in_x)
-
-    first_z = s == 0
-    second_z = s == 1
-    tree = ((act_all, a_first, a_send, a_recv), (sens_all, sn_first, sn_send, sn_recv))
-    for d in range(1, zs):
-        to = 2 * along(first_z, d) + s
-        for buf, first, send, recv in tree:
-            part = buf.at[:, lanes_mine]
-            remote(part, part, send, first.at[d - 1], r, to).start()
-
-    def spread_line(e):
-        lanes = lanes_of(along(first_z, -e))
-        for buf, first, send, recv in tree:
-            part = buf.at[:, lanes]
-            if e > 0:
-                pltpu.make_async_copy(part, part, first.at[e - 1]).wait()
-            for d in range(1, zs):
-                to = 2 * along(second_z, d) + s
-                remote(part, part, send, recv, r, to).start()
-
-    spread_line(0)
+    for e in range(1, zs):
+        spread_line(up_tree, e)
+    for tree in (act_tree, sens_tree):
+        begin(tree)
+        spread_line(tree, 0)
+
+    def bulk(count):
+        blocks = pl.ds(0, count * pair)
+        return ((up_all.at[blocks], u_send, u_recv),) + tuple(
+            (buf.at[:, blocks], send, recv)
+            for buf, send, recv in ((sens_all, sn_send, sn_recv), (act_all, a_send, a_recv))
+        )
 
     def drain_first():
-        for copy in sib_copies:
+        for copy in [sib_up, *sib_copies]:
             copy.wait_send()
-        sent_up = up_all.at[pl.ds(0, (2 * chips - 1) * atoms)]
-        pltpu.make_async_copy(sent_up, sent_up, u_send).wait()
-        for buf, _, send, _ in tree:
-            part = buf.at[:, pl.ds(0, (chips - 1) * pair)]
+        for part, send, _ in bulk(chips - 1):
             pltpu.make_async_copy(part, part, send).wait()
 
     drains.append(drain_first)
@@ -281,9 +274,14 @@
         counts_b[:, k * 128 : (k + 1) * 128] = counts[k].astype(BF16)
 
     for e in range(1, zs):
-        spread_line(e)
-
-    pltpu.make_async_copy(up_all, up_all, u_recv).wait()
+        spread_line(act_tree, e)
+        spread_line(sens_tree, e)
+
+    part, _, recv = bulk(chips - zs)[0]
+    pltpu.make_async_copy(part, part, recv).wait()
+    for d in range(1, rows):
+        to = lax.rem(r + d, rows)
+        pl.semaphore_signal(row_in, inc=1, device_id=(to, c), device_id_type=MESH)
     neighbor_sum = jnp.dot(
         counts_b[...], up_all[...], preferred_element_type=F32
     ) * (1.0 / math.sqrt(nbr))
@@ -328,8 +326,7 @@
         cov_in[j].wait()
         split(j)
 
-    for buf, _, _, recv in tree[::-1]:
-        part = buf.at[:, pl.ds(0, (chips - zs) * pair)]
+    for part, _, recv in bulk(chips - zs)[1:]:
         pltpu.make_async_copy(part, part, recv).wait()
     m0 = lax.broadcasted_iota(jnp.int32, (mg, mg), 0)
     m1 = lax.broadcasted_iota(jnp.int32, (mg, mg), 1)
@@ -486,23 +483,24 @@
     t_mine[...] = jnp.concatenate([part[: mg // 2], part[mg // 2 :]], axis=1)
     t_in[c] = t_mine[...]
 
-    def send_part(k, _):
-        to = lax.rem(c + k, cols)
-        remote(t_mine, t_in.at[c], t_send, t_recv, r, to).start()
-        return 0
-
-    lax.fori_loop(1, cols, send_part, 0)
-
-    def drain_part():
-        sent = t_in.at[pl.ds(0, cols - 1)]
-        pltpu.make_async_copy(sent, sent, t_send).wait()
-
-    drains.append(drain_part)
     swap_n.wait_recv()
     n_wide[...] = jnp.concatenate(
         [n_pair[0].astype(F32), n_pair[1].astype(F32)], axis=1
     ).astype(BF16)
     cast(n_wide, nt_ref, 1)
+
+    def send_part(k, _):
+        to = lax.rem(c + k, cols)
+        remote(t_mine, t_in.at[c], t_send, t_recv, r, to).start()
+        return 0
+
+    lax.fori_loop(1, cols, send_part, 0)
+
+    def drain_part():
+        sent = t_in.at[pl.ds(0, cols - 1)]
+        pltpu.make_async_copy(sent, sent, t_send).wait()
+
+    drains.append(drain_part)
     owned = n_slices.shape[2]
     for t in range(rows):
         n_slices[t] = mine_n[:, t * owned : (t + 1) * owned]
@@ -569,10 +567,18 @@
         drain()
 
 
-def update_kernel(cov_ref, nt_ref, gt_ref, out_ref):
-    out_ref[...] = cov_ref[...] - jnp.dot(
-        gt_ref[...], nt_ref[...], preferred_element_type=F32
-    )
+def update_kernel(parts, cov_ref, nt_ref, gt_ref, out_hbm, made, out_sem):
+    tile = made.shape[0] // parts
+    copies = []
+    for i in range(parts):
+        at = pl.ds(i * tile, tile)
+        made[at, :] = cov_ref[at, :] - jnp.dot(
+            gt_ref[at, :], nt_ref[...], preferred_element_type=F32
+        )
+        copies.append(pltpu.make_async_copy(made.at[at], out_hbm.at[at], out_sem.at[i]))
+        copies[-1].start()
+    for copy in copies:
+        copy.wait()
 
 
 def on_device(
@@ -618,7 +624,6 @@
         out_specs=(vmem,) * 4,
         scratch_shapes=[
             pltpu.VMEM((1, owned), F32),
-            pltpu.VMEM((frames, atoms, adjw), BF16),
             pltpu.VMEM(type_gain.shape, F32),
             pltpu.VMEM((1, mg), jnp.int32),
             pltpu.VMEM((1, measures), F32),
@@ -657,8 +662,9 @@
             dma((10,)),
             dma((zs,)),
             pltpu.SemaphoreType.REGULAR,
-            dma((6,)),
-            dma((6,)),
+            dma((7,)),
+            dma((7,)),
+            dma((zs - 1,)),
             dma,
             dma,
             dma((zs - 1,)),
@@ -708,18 +714,14 @@
             )
         )
     )
-    strip = height // 9
+    parts = width // (8 * math.gcd(width // 8, 9))
     cov_new = pl.pallas_call(
-        update_kernel,
-        grid=(9,),
-        in_specs=[
-            pl.BlockSpec((width, strip), lambda j: (0, j)),
-            pl.BlockSpec((measures, strip), lambda j: (0, j)),
-            pl.BlockSpec((width, measures), lambda j: (0, 0)),
-        ],
-        out_specs=pl.BlockSpec((width, strip), lambda j: (0, j)),
+        functools.partial(update_kernel, parts),
+        in_specs=[vmem] * 3,
+        out_specs=pl.BlockSpec(memory_space=pltpu.HBM),
         out_shape=jax.ShapeDtypeStruct((width, height), F32),
-        compiler_params=pltpu.CompilerParams(vmem_limit_bytes=32 * 2**20),
+        scratch_shapes=[pltpu.VMEM((width, height), F32), dma((parts,))],
+        compiler_params=pltpu.CompilerParams(vmem_limit_bytes=36 * 2**20),
         name="update",
     )(block, n_rows, gain)
     return weights_new.reshape(owned), cov_new.T

time: 64.8 us -> 64.7 us (level)
  the two profiles are of different devices: /device:TPU:5 before, /device:TPU:1 now
where the time goes in v5:
time: 64.7 us; the launch traced here: 64.5 us
  Pallas kernels  63.3 us (98%)
  between operations  0.65 us (1%)
    pallas_call x1, Pallas kernels, on_device(): pl.pallas_call(functools.partial(gain_kernel, rows, cols), out_shape=(jax...  58.8 us
    pallas_call x1, Pallas kernels, on_device(): pl.pallas_call(functools.partial(update_kernel, parts), in_specs=[vmem] *...  4.42 us

profile of v5, /device:TPU:1, one launch (start us, length us, event | category | flops | bytes accessed | tf_op | source)
XLA Modules:
  0.0 64.5 jit_solution(2058369232951394816)
XLA Ops:
  0.6 58.8 %gain.1 = (bf16[64,4608]{1,0:T(8,128)(2,1)S(1)}, bf16[576,64]{1,0:T(8,128)(2,1)S(1)}, f32[1,144]{1,0:T(1,128)S(1)}, f32[576,4608]{1,0:T(8,128)S(1)}) custom-call(f32[576,4608]{1,0:T(8,128)} %bitcast.12, f32[1,144]{1,0:T(1,128)} %bitcast.13, bf16[2,64,144]{2,1,0:T(8,128)(2,1)} %act_hbm.1, bf16[2,64,128]{2,1,0:T(8,128)(2,1)} %up_hbm.1, s32[2,64,138]{2,1,0:T(8,128)} %nb_hbm.1, ...), custom_call_target="tpu_custom_call" | custom-call | tf_op jit(solution)/shard_map/gain/pallas_call | solution.py:615
  59.5 4.4 %update.1 = f32[576,4608]{1,0:T(8,128)} custom-call(f32[576,4608]{1,0:T(8,128)S(1)} %get-tuple-element.7.cov_ref, bf16[64,4608]{1,0:T(8,128)(2,1)S(1)} %get-tuple-element.8.nt_ref, bf16[576,64]{1,0:T(8,128)(2,1)S(1)} %get-tuple-element.9.gt_ref), custom_call_target="tpu_custom_call" | custom-call | tf_op jit(solution)/shard_map/update/pallas_call | solution.py:718
  63.9 0.6 copy.15

commit v6 on v5

--- a/solution.py
+++ b/solution.py
@@ -229,10 +229,11 @@
         act_pair[...].reshape(pair, actw).astype(F32)
     ).astype(BF16)
     sens_all[:, lanes_mine] = jnp.concatenate([sens_pair[0], sens_pair[1]], axis=1)
+    for tree in (act_tree, sens_tree):
+        begin(tree)
     for e in range(1, zs):
         spread_line(up_tree, e)
     for tree in (act_tree, sens_tree):
-        begin(tree)
         spread_line(tree, 0)
 
     def bulk(count):
@@ -269,13 +270,15 @@
             counts[:, pl.ds(row, 1), :] = got.reshape(his, 1, 128)
         return 0
 
-    lax.fori_loop(0, pair // unroll, count, 0)
+    steps = pair // unroll
+    for e in range(zs):
+        if e > 0:
+            spread_line(act_tree, e)
+            spread_line(sens_tree, e)
+        lax.fori_loop(steps * e // zs, steps * (e + 1) // zs, count, 0)
     for k in range(his):
         counts_b[:, k * 128 : (k + 1) * 128] = counts[k].astype(BF16)
 
-    for e in range(1, zs):
-        spread_line(act_tree, e)
-        spread_line(sens_tree, e)
 
     part, _, recv = bulk(chips - zs)[0]
     pltpu.make_async_copy(part, part, recv).wait()
@@ -469,11 +472,6 @@
     n_pair[s] = n_piece[...]
     n_col[r] = n_piece[...]
     for d in range(1, rows):
-        to = lax.rem(r + d, rows)
-        copy = remote(n_piece, n_col.at[r], c_send.at[d - 1], c_recv.at[d - 1], to, c)
-        copy.start()
-        drains.append(copy.wait_send)
-    for d in range(1, rows):
         pltpu.make_async_copy(jac_own, jac_own, j_recv.at[d - 1]).wait()
     n_low = (mine_n - n_piece[...].astype(F32)).astype(BF16)
     jac_here = jac_col[...].reshape(measures, width)
@@ -483,24 +481,29 @@
     t_mine[...] = jnp.concatenate([part[: mg // 2], part[mg // 2 :]], axis=1)
     t_in[c] = t_mine[...]
 
+    def send_part(k, _):
+        to = lax.rem(c + k, cols)
+        remote(t_mine, t_in.at[c], t_send, t_recv, r, to).start()
+        return 0
+
+    lax.fori_loop(1, cols, send_part, 0)
+
+    def drain_part():
+        sent = t_in.at[pl.ds(0, cols - 1)]
+        pltpu.make_async_copy(sent, sent, t_send).wait()
+
+    drains.append(drain_part)
     swap_n.wait_recv()
     n_wide[...] = jnp.concatenate(
         [n_pair[0].astype(F32), n_pair[1].astype(F32)], axis=1
     ).astype(BF16)
     cast(n_wide, nt_ref, 1)
-
-    def send_part(k, _):
-        to = lax.rem(c + k, cols)
-        remote(t_mine, t_in.at[c], t_send, t_recv, r, to).start()
-        return 0
-
-    lax.fori_loop(1, cols, send_part, 0)
-
-    def drain_part():
-        sent = t_in.at[pl.ds(0, cols - 1)]
-        pltpu.make_async_copy(sent, sent, t_send).wait()
-
-    drains.append(drain_part)
+    for d in range(1, rows):
+        to = lax.rem(r + d, rows)
+        copy = remote(n_piece, n_col.at[r], c_send.at[d - 1], c_recv.at[d - 1], to, c)
+        copy.start()
+        drains.append(copy.wait_send)
+
     owned = n_slices.shape[2]
     for t in range(rows):
         n_slices[t] = mine_n[:, t * owned : (t + 1) * owned]

time: 64.7 us -> 59.3 us (0.917)
  Pallas kernels: 63.3 us -> 57.7 us
    pallas_call x1, Pallas kernels: 58.8 us -> 53.2 us  [on_device(): pl.pallas_call(functools.partial(gain_kernel, rows, cols), out_shape=(jax...]
where the time goes in v6:
time: 59.3 us; the launch traced here: 58.9 us
  Pallas kernels  57.7 us (97%)
  between operations  0.65 us (1%)
    pallas_call x1, Pallas kernels, on_device(): pl.pallas_call(functools.partial(gain_kernel, rows, cols), out_shape=(jax...  53.2 us
    pallas_call x1, Pallas kernels, on_device(): pl.pallas_call(functools.partial(update_kernel, parts), in_specs=[vmem] *...  4.41 us

profile of v6, /device:TPU:1, one launch (start us, length us, event | category | flops | bytes accessed | tf_op | source)
XLA Modules:
  0.0 58.9 jit_solution(9957969557502785944)
XLA Ops:
  0.6 53.2 %gain.1 = (bf16[64,4608]{1,0:T(8,128)(2,1)S(1)}, bf16[576,64]{1,0:T(8,128)(2,1)S(1)}, f32[1,144]{1,0:T(1,128)S(1)}, f32[576,4608]{1,0:T(8,128)S(1)}) custom-call(f32[576,4608]{1,0:T(8,128)} %bitcast.12, f32[1,144]{1,0:T(1,128)} %bitcast.13, bf16[2,64,144]{2,1,0:T(8,128)(2,1)} %act_hbm.1, bf16[2,64,128]{2,1,0:T(8,128)(2,1)} %up_hbm.1, s32[2,64,138]{2,1,0:T(8,128)} %nb_hbm.1, ...), custom_call_target="tpu_custom_call" | custom-call | tf_op jit(solution)/shard_map/gain/pallas_call | solution.py:618
  53.9 4.4 %update.1 = f32[576,4608]{1,0:T(8,128)} custom-call(f32[576,4608]{1,0:T(8,128)S(1)} %get-tuple-element.7.cov_ref, bf16[64,4608]{1,0:T(8,128)(2,1)S(1)} %get-tuple-element.8.nt_ref, bf16[576,64]{1,0:T(8,128)(2,1)S(1)} %get-tuple-element.9.gt_ref), custom_call_target="tpu_custom_call" | custom-call | tf_op jit(solution)/shard_map/update/pallas_call | solution.py:721
  58.3 0.6 copy.15

commit v7 on v6

--- a/solution.py
+++ b/solution.py
@@ -176,9 +176,10 @@
         line_mates += [(r, 2 * along(True, d) + s), (r, 2 * along(False, d) + s)]
     for d in range(1, rows):
         line_mates.append((lax.rem(r + d, rows), c))
+    loads[0].start()
     for mate in line_mates:
         pl.semaphore_signal(barrier, inc=1, device_id=mate, device_id_type=MESH)
-    for load in loads + cov_in:
+    for load in loads[1:] + cov_in:
         load.start()
     pl.semaphore_wait(barrier, len(line_mates))
 
@@ -544,9 +545,13 @@
     inverse = eye * first
     left = eye - innovation_cov * first
     for sweep in range(NS_ITERS):
-        inverse = inverse + jnp.dot(inverse, left, precision=FULL, preferred_element_type=F32)
-        if sweep < NS_ITERS - 1:
-            left = jnp.dot(left, left, precision=FULL, preferred_element_type=F32)
+        if sweep == NS_ITERS - 1:
+            both = inverse
+        else:
+            both = jnp.concatenate([inverse, left], axis=0)
+        both = jnp.dot(both, left, precision=FULL, preferred_element_type=F32)
+        inverse = inverse + both[:measures]
+        left = both[measures:]
     for d in range(1, rows):
         pltpu.make_async_copy(n_piece, n_piece, c_recv.at[d - 1]).wait()
     n_cols = n_col[...].reshape(measures, width).astype(F32)

time: 59.3 us -> 59.3 us (level)
  no operation moved by 1% of the time
where the time goes in v7:
time: 59.3 us; the launch traced here: 59 us
  Pallas kernels  57.7 us (97%)
  between operations  0.65 us (1%)
    pallas_call x1, Pallas kernels, on_device(): pl.pallas_call(functools.partial(gain_kernel, rows, cols), out_shape=(jax...  53.3 us
    pallas_call x1, Pallas kernels, on_device(): pl.pallas_call(functools.partial(update_kernel, parts), in_specs=[vmem] *...  4.41 us

profile of v7, /device:TPU:1, one launch (start us, length us, event | category | flops | bytes accessed | tf_op | source)
XLA Modules:
  0.0 59.0 jit_solution(1231044844633485085)
XLA Ops:
  0.6 53.3 %gain.1 = (bf16[64,4608]{1,0:T(8,128)(2,1)S(1)}, bf16[576,64]{1,0:T(8,128)(2,1)S(1)}, f32[1,144]{1,0:T(1,128)S(1)}, f32[576,4608]{1,0:T(8,128)S(1)}) custom-call(f32[576,4608]{1,0:T(8,128)} %bitcast.12, f32[1,144]{1,0:T(1,128)} %bitcast.13, bf16[2,64,144]{2,1,0:T(8,128)(2,1)} %act_hbm.1, bf16[2,64,128]{2,1,0:T(8,128)(2,1)} %up_hbm.1, s32[2,64,138]{2,1,0:T(8,128)} %nb_hbm.1, ...), custom_call_target="tpu_custom_call" | custom-call | tf_op jit(solution)/shard_map/gain/pallas_call | solution.py:623
  54.0 4.4 %update.1 = f32[576,4608]{1,0:T(8,128)} custom-call(f32[576,4608]{1,0:T(8,128)S(1)} %get-tuple-element.7.cov_ref, bf16[64,4608]{1,0:T(8,128)(2,1)S(1)} %get-tuple-element.8.nt_ref, bf16[576,64]{1,0:T(8,128)(2,1)S(1)} %get-tuple-element.9.gt_ref), custom_call_target="tpu_custom_call" | custom-call | tf_op jit(solution)/shard_map/update/pallas_call | solution.py:726
  58.4 0.6 copy.15

commit v8 on v7

--- a/solution.py
+++ b/solution.py
@@ -68,6 +68,7 @@
     jac_own,
     jac_col,
     t_mine,
+    t_other,
     t_in,
     t_rows,
     load_sem,
@@ -480,17 +481,21 @@
         n_piece[...], jac_here, NT, preferred_element_type=F32
     ) + lax.dot_general(n_low, jac_here, NT, preferred_element_type=F32)
     t_mine[...] = jnp.concatenate([part[: mg // 2], part[mg // 2 :]], axis=1)
-    t_in[c] = t_mine[...]
+    swap_t = remote(t_mine, t_other, sib_send.at[7], sib_recv.at[7], r, sib)
+    swap_t.start()
+    drains.append(swap_t.wait_send)
+    swap_t.wait_recv()
+    t_in[h] = t_mine[...] + t_other[...]
 
     def send_part(k, _):
-        to = lax.rem(c + k, cols)
-        remote(t_mine, t_in.at[c], t_send, t_recv, r, to).start()
+        to = 2 * lax.rem(h + k, chips) + s
+        remote(t_in.at[h], t_in.at[h], t_send, t_recv, r, to).start()
         return 0
 
-    lax.fori_loop(1, cols, send_part, 0)
+    lax.fori_loop(1, chips, send_part, 0)
 
     def drain_part():
-        sent = t_in.at[pl.ds(0, cols - 1)]
+        sent = t_in.at[pl.ds(0, chips - 1)]
         pltpu.make_async_copy(sent, sent, t_send).wait()
 
     drains.append(drain_part)
@@ -520,7 +525,7 @@
         def _():
             remote(n_slices.at[t], n_own.at[r], o_send.at[t], o_recv.at[r], x, to).start()
 
-    arrived = t_in.at[pl.ds(0, cols - 1)]
+    arrived = t_in.at[pl.ds(0, chips - 1)]
     pltpu.make_async_copy(arrived, arrived, t_recv).wait()
     t_rows[r] = jnp.sum(t_in[...], axis=0)
     for d in range(1, rows):
@@ -665,13 +670,14 @@
             pltpu.VMEM((mg, width), BF16),
             pltpu.VMEM((rows, mg, width), BF16),
             pltpu.VMEM((mg // 2, 2 * measures), F32),
-            pltpu.VMEM((cols, mg // 2, 2 * measures), F32),
+            pltpu.VMEM((mg // 2, 2 * measures), F32),
+            pltpu.VMEM((chips, mg // 2, 2 * measures), F32),
             pltpu.VMEM((rows, mg // 2, 2 * measures), F32),
             dma((10,)),
             dma((zs,)),
             pltpu.SemaphoreType.REGULAR,
-            dma((7,)),
-            dma((7,)),
+            dma((8,)),
+            dma((8,)),
             dma((zs - 1,)),
             dma,
             dma,

time: 59.3 us -> 59.4 us (level)
  no operation moved by 1% of the time
where the time goes in v8:
time: 59.4 us; the launch traced here: 59.3 us
  Pallas kernels  58.1 us (98%)
  between operations  0.65 us (1%)
    pallas_call x1, Pallas kernels, on_device(): pl.pallas_call(functools.partial(gain_kernel, rows, cols), out_shape=(jax...  53.7 us
    pallas_call x1, Pallas kernels, on_device(): pl.pallas_call(functools.partial(update_kernel, parts), in_specs=[vmem] *...  4.42 us

profile of v8, /device:TPU:1, one launch (start us, length us, event | category | flops | bytes accessed | tf_op | source)
XLA Modules:
  0.0 59.3 jit_solution(13796672702834138149)
XLA Ops:
  0.6 53.7 %gain.1 = (bf16[64,4608]{1,0:T(8,128)(2,1)S(1)}, bf16[576,64]{1,0:T(8,128)(2,1)S(1)}, f32[1,144]{1,0:T(1,128)S(1)}, f32[576,4608]{1,0:T(8,128)S(1)}) custom-call(f32[576,4608]{1,0:T(8,128)} %bitcast.12, f32[1,144]{1,0:T(1,128)} %bitcast.13, bf16[2,64,144]{2,1,0:T(8,128)(2,1)} %act_hbm.1, bf16[2,64,128]{2,1,0:T(8,128)(2,1)} %up_hbm.1, s32[2,64,138]{2,1,0:T(8,128)} %nb_hbm.1, ...), custom_call_target="tpu_custom_call" | custom-call | tf_op jit(solution)/shard_map/gain/pallas_call | solution.py:628
  54.3 4.4 %update.1 = f32[576,4608]{1,0:T(8,128)} custom-call(f32[576,4608]{1,0:T(8,128)S(1)} %get-tuple-element.7.cov_ref, bf16[64,4608]{1,0:T(8,128)(2,1)S(1)} %get-tuple-element.8.nt_ref, bf16[576,64]{1,0:T(8,128)(2,1)S(1)} %get-tuple-element.9.gt_ref), custom_call_target="tpu_custom_call" | custom-call | tf_op jit(solution)/shard_map/update/pallas_call | solution.py:732
  58.7 0.6 copy.15
